TPU v7x, 256 devices: a whole 4x4x8 slice. The times are simulated.
256 devices in a mesh: dp: 64 (over z, x, core), seq: 4 (over y).
Axes of the slice: x: 4, y: 4, z: 8, core: 2. Of those that a mesh axis runs over, the one named last changes fastest.
Arguments:
- x_saved: bfloat16 [32768, 5120], P(('dp', 'seq')), may hold values from -24 to 24
- q_saved: bfloat16 [32768, 2560], P(('dp', 'seq')), may hold values from -8 to 8
- k_saved: bfloat16 [32768, 512], P(('dp', 'seq')), may hold values from -8 to 8
- grad_attn: bfloat16 [32768, 2560], P(('dp', 'seq')), may hold values from -6 to 6
- token_coef: float32 [32768], P(('dp', 'seq')), may hold values from -4 to 4
- dest_of: int32 [32768], P(('dp', 'seq')), may hold values from 0 to 32767, as said below
- source_of: int32 [32768], P(('dp', 'seq')), may hold values from 0 to 32767, as said below
- lengths: int32 [64, 3], P('dp'), may hold values from 64 to 256, as said below
- value_weight: bfloat16 [5120, 512], P('dp'), may hold values from -0.078125 to 0.078125
Outputs:
- grad_x: bfloat16 [32768, 5120], P(('dp', 'seq'))
- grad_q: bfloat16 [32768, 2560], P(('dp', 'seq'))
- grad_k: bfloat16 [32768, 512], P(('dp', 'seq'))
- grad_v_weight: float32 [5120, 512], P('dp')
Inputs may be any that keep to these rules, and one draw needn't show every extreme that they name: dest_of is a permutation that keeps each row at the same index along seq; of the rows of one device, at most 4 go to any one device along dp, and every device sends exactly 4 rows to some device and receives exactly 4 rows from some device. source_of is the inverse permutation of dest_of. The lengths of a group sum to 512; exactly one of them is 256, each other one is at least one eighth of 512.
All inputs are finite; a program needn't handle non-finite values.
Results may differ from a plain program's by a relative error of at most 0.017.
Values may be sent and summed in bfloat16 or wider, within the bound.
No kernel may reach another device: no remote copies, remote signals or barrier semaphores. Data moves between devices by JAX's collectives and lax.ppermute only.
A program may use at most 128 MiB of HBM per device.

v0:
```python
import functools
import math

import jax
import jax.numpy as jnp
from jax import lax
from jax.experimental import pallas as pl
from jax.experimental.pallas import tpu as pltpu
from jax.sharding import PartitionSpec as P

HEAD = 128
CAP = 4
NZ, NX, NC, NS = 8, 4, 2, 4
NDP = NZ * NX * NC
ROWS = 128
GROUP = ROWS * NS
PER = 5
QW = PER * HEAD
BF = jnp.bfloat16
F32 = jnp.float32
SCALE = HEAD ** (-0.5)
LIMIT = 58 * 1024 * 1024

VMEM = pl.BlockSpec(memory_space=pltpu.VMEM)
SMEM = pl.BlockSpec(memory_space=pltpu.SMEM)


def params():
    return pltpu.CompilerParams(vmem_limit_bytes=LIMIT)


def cost(flops, bytes_accessed):
    return pl.CostEstimate(flops=int(flops), bytes_accessed=int(bytes_accessed), transcendentals=0)


def ones_where(hit):
    return jnp.where(hit, 1.0, 0.0).astype(BF)


def mm(a, b):
    return jnp.dot(a, b, preferred_element_type=F32)


def mm_nt(a, b):
    return lax.dot_general(a, b, (((1,), (1,)), ((), ())), preferred_element_type=F32)


def mm_tn(a, b):
    return lax.dot_general(a, b, (((0,), (0,)), ((), ())), preferred_element_type=F32)


def pack_rows_kernel(slots_ref, coef_ref, q_ref, k_ref, g_ref, out_ref):
    row = lax.broadcasted_iota(jnp.int32, (256, ROWS), 0)
    hit = (pl.program_id(0) * 16 + row // 16) * CAP + row % 4 == slots_ref[...]
    place = (row % 16) // 4
    onehot = jnp.concatenate([ones_where(hit & (place == m)) for m in range(4)], axis=1)

    def chunk(s, m):
        if m < PER:
            return q_ref[:, s * QW + m * HEAD : s * QW + (m + 1) * HEAD]
        if m < 2 * PER + 1 and m > PER:
            at = s * QW + (m - PER - 1) * HEAD
            return (coef_ref[...] * g_ref[:, at : at + HEAD].astype(F32)).astype(BF)
        return k_ref[:, s * HEAD : (s + 1) * HEAD]

    for t in range(3):
        rhs = jnp.concatenate(
            [
                jnp.concatenate([chunk(s, 4 * t + m) for m in range(4)], axis=0)
                for s in range(NS)
            ],
            axis=1,
        )
        res = mm(onehot, rhs).astype(BF)
        for s in range(NS):
            out_ref[:, s, 16 * t : 16 * t + 16, :] = res[:, s * HEAD : (s + 1) * HEAD].reshape(
                16, 16, HEAD
            )


def pack_rows(slots, coef, q, k, g):
    return pl.pallas_call(
        pack_rows_kernel,
        grid=(4,),
        out_shape=jax.ShapeDtypeStruct((NDP, NS, 48, HEAD), BF),
        in_specs=[
            pl.BlockSpec((1, ROWS), lambda i: (0, 0)),
            pl.BlockSpec((ROWS, 1), lambda i: (0, 0)),
            pl.BlockSpec((ROWS, NS * QW), lambda i: (0, 0)),
            pl.BlockSpec((ROWS, NS * HEAD), lambda i: (0, 0)),
            pl.BlockSpec((ROWS, NS * QW), lambda i: (0, 0)),
        ],
        out_specs=pl.BlockSpec((16, NS, 48, HEAD), lambda i: (i, 0, 0, 0)),
        compiler_params=params(),
        cost_estimate=cost(1.6e9, 5e6),
        name="pack_rows",
    )(slots, coef, q, k, g)


def values_kernel(place_ref, slot_ref, x_ref, *refs):
    pieces, (out_ref, w_ref) = refs[: NX * NC], refs[NX * NC :]
    at_x0, at_c0 = place_ref[0], place_ref[1]
    block = w_ref.shape[0] // NDP
    for dx in range(NX):
        for dc in range(NC):
            at = lax.rem(at_x0 - dx + NX, NX) * NC + lax.rem(at_c0 + dc, NC)
            for z in range(NZ):
                start = pl.multiple_of((z * NX * NC + at) * block, 16)
                w_ref[pl.ds(start, block), :] = pieces[dx * NC + dc][z]
    row = lax.broadcasted_iota(jnp.int32, (NDP * 16, ROWS), 0)
    wanted = (row // 16) * CAP + row % 4
    of_seq = (row % 16) // 4
    value = mm(x_ref[...], w_ref[...]).astype(BF)
    spread = jnp.concatenate(
        [ones_where((wanted == slot_ref[s : s + 1, :]) & (of_seq == s)) for s in range(NS)],
        axis=1,
    )
    out_ref[...] = mm(spread, value).astype(BF).reshape(NDP, 16, HEAD)


def values_of(place, slots, x_all, pieces):
    return pl.pallas_call(
        values_kernel,
        out_shape=(
            jax.ShapeDtypeStruct((NDP, 16, HEAD), BF),
            jax.ShapeDtypeStruct((x_all.shape[1], HEAD), BF),
        ),
        in_specs=[SMEM] + [VMEM] * (2 + len(pieces)),
        out_specs=(VMEM, VMEM),
        compiler_params=params(),
        cost_estimate=cost(0.8e9, 8e6),
        name="values",
    )(place, slots, x_all, *pieces)


def turn_kernel(x_ref, out_ref):
    out_ref[...] = x_ref[...].T


def turn(x_all):
    depth = x_all.shape[1]
    width = depth // NZ
    return pl.pallas_call(
        turn_kernel,
        grid=(NZ,),
        out_shape=jax.ShapeDtypeStruct((depth, GROUP), BF),
        in_specs=[pl.BlockSpec((GROUP, width), lambda i: (0, i))],
        out_specs=pl.BlockSpec((width, GROUP), lambda i: (i, 0)),
        compiler_params=params(),
        cost_estimate=cost(1e6, 11e6),
        name="turn",
    )(x_all)


def window(s):
    return max(0, s - 2) * ROWS, (s + 1) * ROWS


def probs_kernel(
    len_ref, slot_col_ref, slot_row_ref, r_ref, v_ref, both_out, qs, ks, ds, p0, p1, p2, p3, dv
):
    for s in range(NS):
        lane = lax.broadcasted_iota(jnp.int32, (ROWS, NDP * 16), 1)
        hit = (lane // 16) * CAP + lane % 4 == slot_col_ref[s * ROWS : (s + 1) * ROWS, :]
        place = (lane % 16) // 4
        pick = jnp.concatenate([ones_where(hit & (place == m)) for m in range(4)], axis=0)
        rhs = jnp.concatenate(
            [r_ref[:, s, 16 * t : 16 * t + 16, :].reshape(NDP * 16, HEAD) for t in range(3)],
            axis=1,
        )
        res = mm(pick, rhs).astype(BF)
        qs[s, 0:512, :] = res[:, 0:128]
        qs[s, 512:640, :] = res[0:128, 128:256]
        ks[s * ROWS : (s + 1) * ROWS, :] = res[128:256, 128:256]
        ds[s, 0:256, :] = res[256:512, 128:256]
        ds[s, 256:640, :] = res[0:384, 256:384]

    first, second = len_ref[0], len_ref[0] + len_ref[1]
    dv[...] = jnp.zeros_like(dv)
    for s, p_ref in enumerate((p0, p1, p2, p3)):
        lo, hi = window(s)
        width = hi - lo
        q_pos = s * ROWS + lax.broadcasted_iota(jnp.int32, (ROWS, width), 0)
        k_pos = lo + lax.broadcasted_iota(jnp.int32, (ROWS, width), 1)
        begin = jnp.where(q_pos >= second, second, jnp.where(q_pos >= first, first, 0))
        visible = (k_pos <= q_pos) & (k_pos >= begin)
        scores = mm_nt(qs[s], ks[lo:hi, :]).reshape(PER, ROWS, width) * SCALE
        scores = jnp.where(visible[None], scores, -jnp.inf)
        weights = jnp.exp(scores - jnp.max(scores, axis=2, keepdims=True))
        probs = (weights / jnp.sum(weights, axis=2, keepdims=True)).reshape(PER * ROWS, width)
        p_ref[...] = probs
        dv[lo:hi, :] += mm_tn(probs.astype(BF), ds[s])

    row = lax.broadcasted_iota(jnp.int32, (NDP * 16, ROWS), 0)
    wanted = (row // 16) * CAP + row % 4
    of_seq = (row % 16) // 4
    spread = jnp.concatenate(
        [ones_where((wanted == slot_row_ref[s : s + 1, :]) & (of_seq == s)) for s in range(NS)],
        axis=1,
    )
    both_out[:, 0:16, :] = v_ref[...]
    both_out[:, 16:32, :] = mm(spread, dv[...].astype(BF)).astype(BF).reshape(NDP, 16, HEAD)


def probs_of(lengths, slot_col, slot_row, r, v):
    widths = [window(s)[1] - window(s)[0] for s in range(NS)]
    return pl.pallas_call(
        probs_kernel,
        out_shape=(
            jax.ShapeDtypeStruct((NDP, 32, HEAD), BF),
            jax.ShapeDtypeStruct((NS, PER * ROWS, HEAD), BF),
            jax.ShapeDtypeStruct((GROUP, HEAD), BF),
            jax.ShapeDtypeStruct((NS, PER * ROWS, HEAD), BF),
        )
        + tuple(jax.ShapeDtypeStruct((PER * ROWS, w), F32) for w in widths),
        in_specs=[SMEM, VMEM, VMEM, VMEM, VMEM],
        out_specs=(VMEM,) * 8,
        scratch_shapes=[pltpu.VMEM((GROUP, HEAD), F32)],
        compiler_params=params(),
        cost_estimate=cost(3e9, 9e6),
        name="probs",
    )(lengths, slot_col, slot_row, r, v)


def grads_kernel(
    slot_col_ref, slot_row_ref, r_ref, qs, ks, ds, p0, p1, p2, p3, dqk_out, vs, dq, dk
):
    lane = lax.broadcasted_iota(jnp.int32, (GROUP, NDP * 16), 1)
    row = lax.broadcasted_iota(jnp.int32, (GROUP, NDP * 16), 0)
    hit = ((lane // 16) * CAP + lane % 4 == slot_col_ref[...]) & ((lane % 16) // 4 == row // ROWS)
    vs[...] = mm(ones_where(hit), r_ref[:, 0:16, :].reshape(NDP * 16, HEAD)).astype(BF)
    dk[...] = jnp.zeros_like(dk)
    for s, p_ref in enumerate((p0, p1, p2, p3)):
        lo, hi = window(s)
        probs = p_ref[...]
        dprobs = mm_nt(ds[s], vs[lo:hi, :])
        delta = jnp.sum(probs.astype(BF).astype(F32) * dprobs, axis=1, keepdims=True)
        dscores = (probs * (dprobs - delta)).astype(BF)
        dq[s] = (mm(dscores, ks[lo:hi, :]) * SCALE).astype(BF)
        dk[lo:hi, :] += mm_tn(dscores, qs[s])

    row = lax.broadcasted_iota(jnp.int32, (NDP * 8, ROWS), 0)
    wanted = (row // 8) * CAP + row % 4
    place = (row % 8) // 4
    for s in range(NS):
        hit = wanted == slot_row_ref[s : s + 1, :]
        spread = jnp.concatenate([ones_where(hit & (place == m)) for m in range(2)], axis=1)
        own_k = (dk[s * ROWS : (s + 1) * ROWS, :] * SCALE).astype(BF)
        rhs = jnp.concatenate(
            [
                dq[s, 0:256, :],
                dq[s, 256:512, :],
                jnp.concatenate([dq[s, 512:640, :], own_k], axis=0),
            ],
            axis=1,
        )
        res = mm(spread, rhs)
        for t in range(3):
            dqk_out[:, s, 8 * t : 8 * t + 8, :] = (
                res[:, t * HEAD : (t + 1) * HEAD].reshape(NDP, 8, HEAD).astype(BF)
            )


def grads_of(slot_col, slot_row, r, kept):
    return pl.pallas_call(
        grads_kernel,
        out_shape=jax.ShapeDtypeStruct((NDP, NS, 24, HEAD), BF),
        in_specs=[VMEM] * (3 + len(kept)),
        out_specs=VMEM,
        scratch_shapes=[
            pltpu.VMEM((GROUP, HEAD), BF),
            pltpu.VMEM((NS, PER * ROWS, HEAD), BF),
            pltpu.VMEM((GROUP, HEAD), F32),
        ],
        compiler_params=params(),
        cost_estimate=cost(3e9, 8e6),
        name="grads",
    )(slot_col, slot_row, r, *kept)


def weight_terms_kernel(slot_col_ref, r_ref, x_ref, dv_ref, out_ref):
    @pl.when(pl.program_id(0) == 0)
    def _():
        lane = lax.broadcasted_iota(jnp.int32, (ROWS, NDP * 16), 1)
        wanted = (lane // 16) * CAP + lane % 4
        of_seq = (lane % 16) // 4
        rows = r_ref[:, 16:32, :].reshape(NDP * 16, HEAD)
        for d in range(NS):
            mine = slice(d * ROWS, (d + 1) * ROWS)
            hit = (wanted == slot_col_ref[mine, :]) & (of_seq == d)
            dv_ref[mine, :] = mm(ones_where(hit), rows).astype(BF)

    terms = mm(x_ref[...], dv_ref[...]).astype(BF)
    block = out_ref.shape[3]
    for x in range(NX):
        for c in range(NC):
            at = (x * NC + c) * block
            out_ref[c, x, 0] = terms[at : at + block, :]


def weight_terms(slot_col, r, x_turned):
    block = x_turned.shape[0] // NDP
    return pl.pallas_call(
        weight_terms_kernel,
        grid=(NZ,),
        out_shape=(
            jax.ShapeDtypeStruct((GROUP, HEAD), BF),
            jax.ShapeDtypeStruct((NC, NX, NZ, block, HEAD), BF),
        ),
        in_specs=[
            pl.BlockSpec((GROUP, 1), lambda i: (0, 0)),
            pl.BlockSpec((NDP, 32, HEAD), lambda i: (0, 0, 0)),
            pl.BlockSpec((NX * NC * block, GROUP), lambda i: (i, 0)),
        ],
        out_specs=(
            pl.BlockSpec((GROUP, HEAD), lambda i: (0, 0)),
            pl.BlockSpec((NC, NX, 1, block, HEAD), lambda i: (0, 0, i, 0, 0)),
        ),
        compiler_params=params(),
        cost_estimate=cost(0.8e9, 7e6),
        name="weight_terms",
    )(slot_col, r, x_turned)


def grad_x_kernel(dv_ref, w_ref, out_ref):
    dv = jnp.concatenate([dv_ref[s] for s in range(NS)], axis=1)
    w = jnp.concatenate([w_ref[s] for s in range(NS)], axis=1)
    out_ref[...] = mm_nt(dv, w).astype(BF)


def grad_x_of(dv, w):
    depth = w.shape[1]
    width = 1024
    return pl.pallas_call(
        grad_x_kernel,
        grid=(depth // width,),
        out_shape=jax.ShapeDtypeStruct((ROWS, depth), BF),
        in_specs=[
            pl.BlockSpec((NS, ROWS, HEAD), lambda i: (0, 0, 0)),
            pl.BlockSpec((NS, width, HEAD), lambda i: (0, i, 0)),
        ],
        out_specs=pl.BlockSpec((ROWS, width), lambda i: (0, i)),
        compiler_params=params(),
        cost_estimate=cost(0.7e9, 7e6),
        name="grad_x",
    )(dv, w)


def unpack_kernel(slot_col_ref, r_ref, q_ref, k_ref):
    lane = lax.broadcasted_iota(jnp.int32, (ROWS, NDP * 8), 1)
    hit = (lane // 8) * CAP + lane % 4 == slot_col_ref[...]
    place = (lane % 8) // 4
    pick = jnp.concatenate([ones_where(hit & (place == m)) for m in range(2)], axis=0)
    for s in range(NS):
        rhs = jnp.concatenate(
            [
                r_ref[:, s, 8 * t : 8 * t + 8, :].astype(F32).reshape(NDP * 8, HEAD).astype(BF)
                for t in range(3)
            ],
            axis=1,
        )
        res = mm(pick, rhs).astype(BF)
        for m in range(PER):
            t, at = m // 2, (m % 2) * ROWS
            q_ref[:, s * QW + m * HEAD : s * QW + (m + 1) * HEAD] = res[
                at : at + ROWS, t * HEAD : (t + 1) * HEAD
            ]
        k_ref[:, s * HEAD : (s + 1) * HEAD] = res[ROWS : 2 * ROWS, 2 * HEAD : 3 * HEAD]


def unpack(slot_col, r):
    return pl.pallas_call(
        unpack_kernel,
        out_shape=(
            jax.ShapeDtypeStruct((ROWS, NS * QW), BF),
            jax.ShapeDtypeStruct((ROWS, NS * HEAD), BF),
        ),
        in_specs=[VMEM, VMEM],
        out_specs=(VMEM, VMEM),
        compiler_params=params(),
        cost_estimate=cost(0.5e9, 4e6),
        name="unpack",
    )(slot_col, r)


def dp_of(z, x, c):
    return (z * NX + x) * NC + c


EACH = [(z, x, c) for z in range(NZ) for x in range(NX) for c in range(NC)]


def along_z(value, d):
    return lax.ppermute(value, "dp", [(dp_of(z, x, c), dp_of((z + d) % NZ, x, c)) for z, x, c in EACH])


def along_x(value, d):
    return lax.ppermute(value, "dp", [(dp_of(z, x, c), dp_of(z, (x + d) % NX, c)) for z, x, c in EACH])


def along_c(value):
    return lax.ppermute(value, "dp", [(dp_of(z, x, c), dp_of(z, x, 1 - c)) for z, x, c in EACH])


def along_seq(value, d):
    return lax.ppermute(value, "seq", [(s, (s + d) % NS) for s in range(NS)])


def rank_of(label, key):
    same = (label[:, None] == label[None, :]) & (key[None, :] < key[:, None])
    return jnp.sum(same.astype(jnp.int32), axis=1)


def in_order(parts, own):
    count = len(parts)
    index = jnp.arange(count, dtype=jnp.int32).reshape((count,) + (1,) * parts[0].ndim)
    total = jnp.zeros((count,) + parts[0].shape, parts[0].dtype)
    for d, part in enumerate(parts):
        total = jnp.where(index == (own - d) % count, part[None], total)
    return total


def shards(
    x_saved, q_saved, k_saved, grad_attn, token_coef, dest_of, source_of, lengths, value_weight
):
    dp, seq = lax.axis_index("dp"), lax.axis_index("seq")
    z, x, c = dp // (NX * NC), (dp // NC) % NX, dp % NC

    def pick(value, at):
        return lax.dynamic_index_in_dim(value, at, 0, keepdims=False)

    target = dest_of // GROUP
    send_slot = target * CAP + rank_of(target, jnp.arange(ROWS, dtype=jnp.int32))
    anchor = source_of // GROUP
    recv_slot = anchor * CAP + rank_of(anchor, source_of)
    slots = jnp.stack([send_slot, recv_slot])

    stage = lax.dynamic_slice_in_dim(value_weight, seq * HEAD, HEAD, axis=1)[None]
    for bit in (1, 2, 4):
        swap = [(dp_of(a, b, e), dp_of(a ^ bit, b, e)) for a, b, e in EACH]
        other = lax.ppermute(stage, "dp", swap)
        mine = (z // bit) % 2 == 0
        stage = jnp.concatenate(
            [jnp.where(mine, stage, other), jnp.where(mine, other, stage)], axis=0
        )

    rows = pack_rows(send_slot[None], token_coef[:, None], q_saved, k_saved, grad_attn)
    rows, slots, stage = lax.optimization_barrier((rows, slots, stage))
    arrived = lax.all_to_all(
        rows.reshape(NDP * NS, 48, HEAD), ("dp", "seq"), split_axis=0, concat_axis=0, tiled=True
    )
    slot_parts = [slots] + [along_seq(slots, d) for d in range(1, NS)]
    all_slots = in_order(slot_parts, seq)
    send_all, recv_all = all_slots[:, 0], all_slots[:, 1]
    send_col, recv_col = send_all.reshape(GROUP, 1), recv_all.reshape(GROUP, 1)
    own_col = send_slot[:, None]
    pieces = []
    for part in [stage] + [along_x(stage, d) for d in range(1, NX)]:
        pieces += [part, along_c(part)]
    x_all = lax.all_gather(x_saved, "seq", axis=0, tiled=True)
    place = jnp.stack([x, c]).astype(jnp.int32)
    v_out, head_w = values_of(place, send_all, x_all, pieces)
    w_all = lax.all_gather(head_w, "seq", axis=0, tiled=True)
    arrived, send_col, recv_col, own_col, v_out = lax.optimization_barrier(
        (arrived, send_col, recv_col, own_col, v_out)
    )

    both, *kept = probs_of(
        lengths[0], recv_col, recv_all, arrived.reshape(NDP, NS, 48, HEAD), v_out
    )

    both = lax.all_to_all(both, "dp", split_axis=0, concat_axis=0, tiled=True)
    x_turned = turn(x_all)
    both, x_turned = lax.optimization_barrier((both, x_turned))
    dqk_out = grads_of(recv_col, recv_all, both, kept)
    dqk_out, send_col = lax.optimization_barrier((dqk_out, send_col))
    dv_head, terms = weight_terms(send_col, both, x_turned)

    dqk_back = lax.all_to_all(
        dqk_out.reshape(NDP * NS, 24, HEAD), ("dp", "seq"), split_axis=0, concat_axis=0, tiled=True
    )

    part = pick(terms, c).astype(F32) + along_c(pick(terms, 1 - c)).astype(F32)
    part = part.astype(BF)
    total = pick(part, x).astype(F32)
    for d in range(1, NX):
        total = total + along_x(pick(part, (x + d) % NX), d).astype(F32)
    dv_view = dv_head.reshape(NS, ROWS, HEAD)
    dv_parts = [pick(dv_view, seq)]
    for d in range(1, NS):
        dv_parts.append(along_seq(pick(dv_view, (seq + d) % NS), d))
    grad_x = grad_x_of(in_order(dv_parts, seq), w_all.reshape(NS, -1, HEAD))

    total, grad_x, dqk_back = lax.optimization_barrier((total, grad_x, dqk_back))
    for bit in (1, 2, 4):
        half = total.astype(BF)
        count = half.shape[0]
        view = half.reshape(count // 2, 2, *half.shape[1:])
        mine = (z // bit) % 2
        swap = [
            (dp_of(a, b, e), dp_of(a ^ bit, b, e)) for a, b, e in EACH
        ]
        keep = lax.dynamic_index_in_dim(view, mine, 1, keepdims=False)
        give = lax.dynamic_index_in_dim(view, 1 - mine, 1, keepdims=False)
        total = keep.astype(F32) + lax.ppermute(give, "dp", swap).astype(F32)
    own = total[0] / math.sqrt(GROUP * NDP)
    heads = in_order([own] + [along_seq(own, d) for d in range(1, NS)], seq)
    grad_v_weight = jnp.concatenate([heads[s] for s in range(NS)], axis=1)

    grad_q, grad_k = unpack(own_col, dqk_back.reshape(NDP, NS, 24, HEAD))
    return (grad_x, grad_q, grad_k, grad_v_weight)


def solution(mesh):
    rows = P(("dp", "seq"), None)
    flat = P(("dp", "seq"))
    whole = P("dp", None)
    return jax.shard_map(
        shards,
        mesh=mesh,
        in_specs=(rows, rows, rows, rows, flat, flat, flat, whole, whole),
        out_specs=(rows, rows, rows, whole),
        check_vma=False,
    )
```

profile of v0, /device:TPU:32, one launch (start us, length us, event | category | flops | bytes accessed | tf_op | source)
XLA Modules:
  0.0 240.5 jit_solution(14326886130066589161)
XLA Ops:
  11.9 3.4 %collective-permute-start.1 = (bf16[2,80,128]{2,1,0:T(8,128)(2,1)S(1)}, bf16[2,80,128]{2,1,0:T(8,128)(2,1)S(1)}, u32[]{:S(2)}, u32[]{:S(2)}) collective-permute-start(bf16[2,80,128]{2,1,0:T(8,128)(2,1)S(1)} %pad_maximum_fusion.3), channel_id=1, source_target_pairs={{0,64},{4,68},{8,72},{12,76},{16,80},{20,84},{24,88},{28,92},{32,9... | collective-permute-start | bytes 122888 | tf_op jit(solution)/shard_map/ppermute | solution.py:441
  15.2 5.0 %pack_rows.1 = bf16[64,4,48,128]{3,2,1,0:T(8,128)(2,1)} custom-call(s32[1,128]{1,0:T(1,128)} %get-tuple-element.84.slots_ref, f32[128,1]{1,0:T(8,128)} %copy.24.coef_ref, bf16[128,2560]{1,0:T(8,128)(2,1)} %q_ref.1, bf16[128,512]{1,0:T(8,128)(2,1)} %k_ref.1, bf16[128,2560]{1,0:T(8,128)(2,1)} %g_ref.1), custom_call_target="tpu_custom_call" | custom-call | flops 1600000000 | bytes 5000000 | tf_op jit(solution)/shard_map/pack_rows/pallas_call | solution.py:82
  20.3 4.6 %collective-permute-start.2 = (bf16[4,80,128]{2,1,0:T(8,128)(2,1)S(1)}, bf16[4,80,128]{2,1,0:T(8,128)(2,1)S(1)}, u32[]{:S(2)}, u32[]{:S(2)}) collective-permute-start(bf16[4,80,128]{2,1,0:T(8,128)(2,1)S(1)} %pad_maximum_fusion.2), channel_id=1, source_target_pairs={{0,128},{4,132},{8,136},{12,140},{16,144},{20,148},{24,152},{28,15... | collective-permute-start | bytes 245768 | tf_op jit(solution)/shard_map/ppermute | solution.py:441
  24.9 4.3 %collective-permute-done.2 = bf16[4,80,128]{2,1,0:T(8,128)(2,1)S(1)} collective-permute-done((bf16[4,80,128]{2,1,0:T(8,128)(2,1)S(1)}, bf16[4,80,128]{2,1,0:T(8,128)(2,1)S(1)}, u32[]{:S(2)}, u32[]{:S(2)}) %collective-permute-start.2) | collective-permute-done | bytes 81952 | tf_op jit(solution)/shard_map/ppermute | solution.py:441
  29.2 12.1 %all-to-all-start = ((bf16[256,48,128]{2,1,0:T(8,128)(2,1)}), bf16[256,48,128]{2,1,0:T(8,128)(2,1)S(1)}, u32[]{:S(2)}, u32[]{:S(2)}) async-start(bf16[256,48,128]{2,1,0:T(8,128)(2,1)} %bitcast.73), calls=%async_computation | async-start | bytes 6291456 | tf_op jit(solution)/shard_map/all_to_all | solution.py:449
  46.8 3.0 %collective-permute-start.9 = (bf16[8,80,128]{2,1,0:T(8,128)(2,1)S(1)}, bf16[8,80,128]{2,1,0:T(8,128)(2,1)S(1)}, u32[]{:S(2)}, u32[]{:S(2)}) collective-permute-start(bf16[8,80,128]{2,1,0:T(8,128)(2,1)S(1)} %pad_maximum_fusion.refs_0_), channel_id=1, source_target_pairs={{0,16},{4,20},{8,24},{12,28},{16,0},{20,4},{24,8},{28,12},{32,48},... | collective-permute-start | bytes 491528 | tf_op jit(solution)/shard_map/ppermute | solution.py:398
  52.3 4.2 %collective-permute-done.9.refs_4_ = bf16[8,80,128]{2,1,0:T(8,128)(2,1)S(1)} collective-permute-done((bf16[8,80,128]{2,1,0:T(8,128)(2,1)S(1)}, bf16[8,80,128]{2,1,0:T(8,128)(2,1)S(1)}, u32[]{:S(2)}, u32[]{:S(2)}) %collective-permute-start.9) | collective-permute-done | bytes 163872 | tf_op jit(solution)/shard_map/ppermute | solution.py:398
  56.5 6.7 %collective-permute-done.11.refs_6_ = bf16[8,80,128]{2,1,0:T(8,128)(2,1)S(1)} collective-permute-done((bf16[8,80,128]{2,1,0:T(8,128)(2,1)S(1)}, bf16[8,80,128]{2,1,0:T(8,128)(2,1)S(1)}, u32[]{:S(2)}, u32[]{:S(2)}) %collective-permute-start.11) | collective-permute-done | bytes 163872 | tf_op jit(solution)/shard_map/ppermute | solution.py:398
  66.5 32.6 %all-gather.3.cloned.1.call-done.x_ref = bf16[512,5120]{1,0:T(8,128)(2,1)} async-done(((bf16[128,5120]{1,0:T(8,128)(2,1)}), bf16[512,5120]{1,0:T(8,128)(2,1)}) %all-gather.3.cloned.1.call-update) | async-done | bytes 5242896 | tf_op jit(solution)/shard_map/all_gather | solution.py:460
  99.1 6.0 %values.1 = (bf16[64,16,128]{2,1,0:T(8,128)(2,1)}, bf16[5120,128]{1,0:T(8,128)(2,1)}) custom-call(s32[2]{0:T(128)} %pad_add_fusion.1.place_ref, s32[4,128]{1,0:T(4,128)} %get-tuple-element.80.slot_ref, bf16[512,5120]{1,0:T(8,128)(2,1)} %all-gather.3.cloned.1.call-done.x_ref, bf16[8,80,128]{2,1,0:T(8,128)(2,1)} %copy-done.4, bf16[8,80,128]{2,1,0:T(8,128)(2,1)} %copy-done.8, ...), custom_call_target="tpu_custom_call" | custom-call | flops 800000000 | bytes 8000000 | tf_op jit(solution)/shard_map/values/pallas_call | solution.py:122
  105.2 11.0 %all-to-all-done = bf16[256,48,128]{2,1,0:T(8,128)(2,1)S(1)} async-done(((bf16[256,48,128]{2,1,0:T(8,128)(2,1)}), bf16[256,48,128]{2,1,0:T(8,128)(2,1)S(1)}, u32[]{:S(2)}, u32[]{:S(2)}) %all-to-all-start) | async-done | bytes 3145760 | tf_op jit(solution)/shard_map/all_to_all | solution.py:449
  118.0 8.0 %probs.1 = (bf16[64,32,128]{2,1,0:T(8,128)(2,1)}, bf16[4,640,128]{2,1,0:T(8,128)(2,1)}, bf16[512,128]{1,0:T(8,128)(2,1)}, bf16[4,640,128]{2,1,0:T(8,128)(2,1)}, ...) custom-call(s32[3]{0:T(128)} %bitcast.85, s32[512,1]{1,0:T(8,128)} %copy.26.slot_col_ref, ...), custom_call_target="tpu_custom_call" | custom-call | flops 3000000000 | bytes 9000000 | tf_op jit(solution)/shard_map/probs/pallas_call | solution.py:207
  126.0 6.3 %all-to-all-start.1 = ((bf16[64,32,128]{2,1,0:T(8,128)(2,1)}), bf16[64,32,128]{2,1,0:T(8,128)(2,1)S(1)}, u32[]{:S(2)}, u32[]{:S(2)}) async-start(bf16[64,32,128]{2,1,0:T(8,128)(2,1)} %get-tuple-element.40), calls=%async_computation.1 | async-start | bytes 1048576 | tf_op jit(solution)/shard_map/all_to_all | solution.py:472
  132.3 7.8 %turn.1.x_ref = bf16[5120,512]{1,0:T(8,128)(2,1)} custom-call(bf16[512,5120]{1,0:T(8,128)(2,1)} %all-gather.3.cloned.1.call-done.x_ref), custom_call_target="tpu_custom_call" | custom-call | flops 1000000 | bytes 11000000 | tf_op jit(solution)/shard_map/turn/pallas_call | solution.py:143
  140.1 8.9 %all-to-all-done.1.r_ref = bf16[64,32,128]{2,1,0:T(8,128)(2,1)S(1)} async-done(((bf16[64,32,128]{2,1,0:T(8,128)(2,1)}), bf16[64,32,128]{2,1,0:T(8,128)(2,1)S(1)}, u32[]{:S(2)}, u32[]{:S(2)}) %all-to-all-start.1) | async-done | bytes 524320 | tf_op jit(solution)/shard_map/all_to_all | solution.py:472
  149.8 7.1 %grads.1 = bf16[64,4,24,128]{3,2,1,0:T(8,128)(2,1)} custom-call(s32[512,1]{1,0:T(8,128)} %copy.26.slot_col_ref, s32[4,128]{1,0:T(4,128)} %get-tuple-element.79.slot_row_ref, bf16[64,32,128]{2,1,0:T(8,128)(2,1)} %copy-done.1, bf16[4,640,128]{2,1,0:T(8,128)(2,1)} %get-tuple-element.42.qs, bf16[512,128]{1,0:T(8,128)(2,1)} %get-tuple-element.43.ks, ...), custom_call_target="tpu_custom_call" | custom-call | flops 3000000000 | bytes 8000000 | tf_op jit(solution)/shard_map/grads/pallas_call | solution.py:265
  156.9 8.0 %all-to-all-start.2 = ((bf16[256,24,128]{2,1,0:T(8,128)(2,1)}), bf16[256,24,128]{2,1,0:T(8,128)(2,1)S(1)}, u32[]{:S(2)}, u32[]{:S(2)}) async-start(bf16[256,24,128]{2,1,0:T(8,128)(2,1)} %bitcast.76), calls=%async_computation.2 | async-start | bytes 3145728 | tf_op jit(solution)/shard_map/all_to_all | solution.py:479
  165.8 8.1 %weight_terms.1 = (bf16[512,128]{1,0:T(8,128)(2,1)}, bf16[2,4,8,80,128]{4,3,2,1,0:T(8,128)(2,1)}) custom-call(s32[512,1]{1,0:T(8,128)} %copy.27.slot_col_ref, bf16[64,32,128]{2,1,0:T(8,128)(2,1)} %copy-done.1, bf16[5120,512]{1,0:T(8,128)(2,1)} %turn.1.x_ref), custom_call_target="tpu_custom_call" | custom-call | flops 800000000 | bytes 7000000 | tf_op jit(solution)/shard_map/weight_terms/pallas_call | solution.py:303
  188.2 5.7 %collective-permute-done.14 = bf16[8,80,128]{2,1,0:T(8,128)(2,1)S(1)} collective-permute-done((bf16[8,80,128]{2,1,0:T(8,128)(2,1)S(1)}, bf16[8,80,128]{2,1,0:T(8,128)(2,1)S(1)}, u32[]{:S(2)}, u32[]{:S(2)}) %collective-permute-start.14) | collective-permute-done | bytes 163872 | tf_op jit(solution)/shard_map/ppermute | solution.py:398
  193.9 5.2 %collective-permute-done.15 = bf16[8,80,128]{2,1,0:T(8,128)(2,1)S(1)} collective-permute-done((bf16[8,80,128]{2,1,0:T(8,128)(2,1)S(1)}, bf16[8,80,128]{2,1,0:T(8,128)(2,1)S(1)}, u32[]{:S(2)}, u32[]{:S(2)}) %collective-permute-start.15) | collective-permute-done | bytes 163872 | tf_op jit(solution)/shard_map/ppermute | solution.py:398
  199.3 6.1 %grad_x.1 = bf16[128,5120]{1,0:T(8,128)(2,1)} custom-call(bf16[4,128,128]{2,1,0:T(8,128)(2,1)} %select_select_fusion.1.dv_ref, bf16[4,5120,128]{2,1,0:T(8,128)(2,1)} %bitcast.72), custom_call_target="tpu_custom_call" | custom-call | flops 700000000 | bytes 7000000 | tf_op jit(solution)/shard_map/grad_x/pallas_call | solution.py:334
  206.9 4.1 %collective-permute-done.20 = bf16[4,80,128]{2,1,0:T(8,128)(2,1)S(1)} collective-permute-done((bf16[4,80,128]{2,1,0:T(8,128)(2,1)S(1)}, bf16[4,80,128]{2,1,0:T(8,128)(2,1)S(1)}, u32[]{:S(2)}, u32[]{:S(2)}) %collective-permute-start.20) | collective-permute-done | bytes 81952 | tf_op jit(solution)/shard_map/ppermute | solution.py:505
  216.0 4.4 %collective-permute-start.22 = (bf16[1,80,128]{2,1,0:T(8,128)(2,1)S(1)}, bf16[1,80,128]{2,1,0:T(8,128)(2,1)S(1)}, u32[]{:S(2)}, u32[]{:S(2)}) collective-permute-start(bf16[1,80,128]{2,1,0:T(8,128)(2,1)S(1)} %constant_dynamic-slice_fusion), channel_id=1, source_target_pairs={{0,128},{4,132},{8,136},{12,140},{16,144},{20,148},{24,152},{28,15... | collective-permute-start | bytes 61448 | tf_op jit(solution)/shard_map/ppermute | solution.py:505
  227.7 3.1 %unpack.1 = (bf16[128,2560]{1,0:T(8,128)(2,1)}, bf16[128,512]{1,0:T(8,128)(2,1)}) custom-call(s32[128,1]{1,0:T(8,128)} %copy.28.slot_col_ref, bf16[64,4,24,128]{3,2,1,0:T(8,128)(2,1)} %bitcast.75), custom_call_target="tpu_custom_call" | custom-call | flops 500000000 | bytes 4000000 | tf_op jit(solution)/shard_map/unpack/pallas_call | solution.py:372
  (119 shorter events, 50.4 us)
Async XLA Ops:
  7.2 91.9 %all-gather.3.cloned.1.call-start = ((), (), s32[]{:S(2)}) async-start(), calls=%async_computation.3 | async-start | bytes 6553600 | tf_op jit(solution)/shard_map/all_gather | solution.py:460
  11.9 8.3 %collective-permute-start.1 = (bf16[2,80,128]{2,1,0:T(8,128)(2,1)S(1)}, bf16[2,80,128]{2,1,0:T(8,128)(2,1)S(1)}, u32[]{:S(2)}, u32[]{:S(2)}) collective-permute-start(bf16[2,80,128]{2,1,0:T(8,128)(2,1)S(1)} %pad_maximum_fusion.3), channel_id=1, source_target_pairs={{0,64},{4,68},{8,72},{12,76},{16,80},{20,84},{24,88},{28,92},{32,9... | collective-permute-start | bytes 122888 | tf_op jit(solution)/shard_map/ppermute | solution.py:441
  20.3 8.9 %collective-permute-start.2 = (bf16[4,80,128]{2,1,0:T(8,128)(2,1)S(1)}, bf16[4,80,128]{2,1,0:T(8,128)(2,1)S(1)}, u32[]{:S(2)}, u32[]{:S(2)}) collective-permute-start(bf16[4,80,128]{2,1,0:T(8,128)(2,1)S(1)} %pad_maximum_fusion.2), channel_id=1, source_target_pairs={{0,128},{4,132},{8,136},{12,140},{16,144},{20,148},{24,152},{28,15... | collective-permute-start | bytes 245768 | tf_op jit(solution)/shard_map/ppermute | solution.py:441
  29.2 86.9 %all-to-all-start = ((bf16[256,48,128]{2,1,0:T(8,128)(2,1)}), bf16[256,48,128]{2,1,0:T(8,128)(2,1)S(1)}, u32[]{:S(2)}, u32[]{:S(2)}) async-start(bf16[256,48,128]{2,1,0:T(8,128)(2,1)} %bitcast.73), calls=%async_computation | async-start | bytes 6291456 | tf_op jit(solution)/shard_map/all_to_all | solution.py:449
  41.4 157.9 %all-gather.5.cloned.1.call-start = ((), (), s32[]{:S(2)}) async-start(), calls=%async_computation.4 | async-start | bytes 6553600 | tf_op jit(solution)/shard_map/all_gather | solution.py:463
  41.5 9.4 %collective-permute-start.3 = (s32[2,128]{1,0:T(2,128)S(1)}, s32[2,128]{1,0:T(2,128)S(1)}, u32[]{:S(2)}, u32[]{:S(2)}) collective-permute-start(s32[2,128]{1,0:T(2,128)S(1)} %pad_add_fusion), channel_id=1, source_target_pairs={{0,3},{1,0},{2,1},{3,2},{4,7},{5,4},{6,5},{7,6},{8,11},{9,8},{10,9... | collective-permute-start | bytes 3080 | tf_op jit(solution)/shard_map/ppermute | solution.py:406
  44.5 7.7 %collective-permute-start.4 = (s32[2,128]{1,0:T(2,128)S(1)}, s32[2,128]{1,0:T(2,128)S(1)}, u32[]{:S(2)}, u32[]{:S(2)}) collective-permute-start(s32[2,128]{1,0:T(2,128)S(1)} %pad_add_fusion), channel_id=1, source_target_pairs={{0,2},{1,3},{2,0},{3,1},{4,6},{5,7},{6,4},{7,5},{8,10},{9,11},{10,... | collective-permute-start | bytes 3080 | tf_op jit(solution)/shard_map/ppermute | solution.py:406
  45.2 7.0 %collective-permute-start.5 = (s32[2,128]{1,0:T(2,128)S(1)}, s32[2,128]{1,0:T(2,128)S(1)}, u32[]{:S(2)}, u32[]{:S(2)}) collective-permute-start(s32[2,128]{1,0:T(2,128)S(1)} %pad_add_fusion), channel_id=1, source_target_pairs={{0,1},{1,2},{2,3},{3,0},{4,5},{5,6},{6,7},{7,4},{8,9},{9,10},{10,1... | collective-permute-start | bytes 3080 | tf_op jit(solution)/shard_map/ppermute | solution.py:406
  46.8 9.7 %collective-permute-start.9 = (bf16[8,80,128]{2,1,0:T(8,128)(2,1)S(1)}, bf16[8,80,128]{2,1,0:T(8,128)(2,1)S(1)}, u32[]{:S(2)}, u32[]{:S(2)}) collective-permute-start(bf16[8,80,128]{2,1,0:T(8,128)(2,1)S(1)} %pad_maximum_fusion.refs_0_), channel_id=1, source_target_pairs={{0,16},{4,20},{8,24},{12,28},{16,0},{20,4},{24,8},{28,12},{32,48},... | collective-permute-start | bytes 491528 | tf_op jit(solution)/shard_map/ppermute | solution.py:398
  49.8 13.5 %collective-permute-start.11 = (bf16[8,80,128]{2,1,0:T(8,128)(2,1)S(1)}, bf16[8,80,128]{2,1,0:T(8,128)(2,1)S(1)}, u32[]{:S(2)}, u32[]{:S(2)}) collective-permute-start(bf16[8,80,128]{2,1,0:T(8,128)(2,1)S(1)} %pad_maximum_fusion.refs_0_), channel_id=1, source_target_pairs={{0,24},{4,28},{8,0},{12,4},{16,8},{20,12},{24,16},{28,20},{32,56},... | collective-permute-start | bytes 491528 | tf_op jit(solution)/shard_map/ppermute | solution.py:398
  50.9 13.5 %collective-permute-start.7 = (bf16[8,80,128]{2,1,0:T(8,128)(2,1)S(1)}, bf16[8,80,128]{2,1,0:T(8,128)(2,1)S(1)}, u32[]{:S(2)}, u32[]{:S(2)}) collective-permute-start(bf16[8,80,128]{2,1,0:T(8,128)(2,1)S(1)} %pad_maximum_fusion.refs_0_), channel_id=1, source_target_pairs={{0,8},{4,12},{8,16},{12,20},{16,24},{20,28},{24,0},{28,4},{32,40},... | collective-permute-start | bytes 491528 | tf_op jit(solution)/shard_map/ppermute | solution.py:398
  52.2 13.0 %collective-permute-start.6 = (bf16[8,80,128]{2,1,0:T(8,128)(2,1)S(1)}, bf16[8,80,128]{2,1,0:T(8,128)(2,1)S(1)}, u32[]{:S(2)}, u32[]{:S(2)}) collective-permute-start(bf16[8,80,128]{2,1,0:T(8,128)(2,1)S(1)} %pad_maximum_fusion.refs_0_), channel_id=1, source_target_pairs={{0,4},{4,0},{8,12},{12,8},{16,20},{20,16},{24,28},{28,24},{32,36},... | collective-permute-start | bytes 491528 | tf_op jit(solution)/shard_map/ppermute | solution.py:402
  56.5 8.6 %collective-permute-start.10 = (bf16[8,80,128]{2,1,0:T(8,128)(2,1)S(1)}, bf16[8,80,128]{2,1,0:T(8,128)(2,1)S(1)}, u32[]{:S(2)}, u32[]{:S(2)}) collective-permute-start(bf16[8,80,128]{2,1,0:T(8,128)(2,1)S(1)} %collective-permute-done.9.refs_4_), channel_id=1, source_target_pairs={{0,4},{4,0},{8,12},{12,8},{16,20},{20,16},{24,28},{28,24},{32,36},... | collective-permute-start | bytes 491528 | tf_op jit(solution)/shard_map/ppermute | solution.py:402
  126.0 23.1 %all-to-all-start.1 = ((bf16[64,32,128]{2,1,0:T(8,128)(2,1)}), bf16[64,32,128]{2,1,0:T(8,128)(2,1)S(1)}, u32[]{:S(2)}, u32[]{:S(2)}) async-start(bf16[64,32,128]{2,1,0:T(8,128)(2,1)} %get-tuple-element.40), calls=%async_computation.1 | async-start | bytes 1048576 | tf_op jit(solution)/shard_map/all_to_all | solution.py:472
  156.9 49.4 %all-to-all-start.2 = ((bf16[256,24,128]{2,1,0:T(8,128)(2,1)}), bf16[256,24,128]{2,1,0:T(8,128)(2,1)S(1)}, u32[]{:S(2)}, u32[]{:S(2)}) async-start(bf16[256,24,128]{2,1,0:T(8,128)(2,1)} %bitcast.76), calls=%async_computation.2 | async-start | bytes 3145728 | tf_op jit(solution)/shard_map/all_to_all | solution.py:479
  175.9 5.6 %collective-permute-start.13 = (bf16[4,8,80,128]{3,2,1,0:T(8,128)(2,1)}, bf16[4,8,80,128]{3,2,1,0:T(8,128)(2,1)S(1)}, u32[]{:S(2)}, u32[]{:S(2)}) collective-permute-start(bf16[4,8,80,128]{3,2,1,0:T(8,128)(2,1)} %dynamic-slice_bitcast_fusion), channel_id=1, source_target_pairs={{0,4},{4,0},{8,12},{12,8},{16,20},{20,16},{24,28},{28,24},{32,36},... | collective-permute-start | bytes 1966088 | tf_op jit(solution)/shard_map/ppermute | solution.py:402
  176.9 9.1 %collective-permute-start.17 = (bf16[128,128]{1,0:T(8,128)(2,1)S(1)}, bf16[128,128]{1,0:T(8,128)(2,1)S(1)}, u32[]{:S(2)}, u32[]{:S(2)}) collective-permute-start(bf16[128,128]{1,0:T(8,128)(2,1)S(1)} %get-tuple-element.71), channel_id=1, source_target_pairs={{0,3},{1,0},{2,1},{3,2},{4,7},{5,4},{6,5},{7,6},{8,11},{9,8},{10,9... | collective-permute-start | bytes 98312 | tf_op jit(solution)/shard_map/ppermute | solution.py:406
  179.9 7.6 %collective-permute-start.18 = (bf16[128,128]{1,0:T(8,128)(2,1)S(1)}, bf16[128,128]{1,0:T(8,128)(2,1)S(1)}, u32[]{:S(2)}, u32[]{:S(2)}) collective-permute-start(bf16[128,128]{1,0:T(8,128)(2,1)S(1)} %get-tuple-element.74), channel_id=1, source_target_pairs={{0,2},{1,3},{2,0},{3,1},{4,6},{5,7},{6,4},{7,5},{8,10},{9,11},{10,... | collective-permute-start | bytes 98312 | tf_op jit(solution)/shard_map/ppermute | solution.py:406
  180.6 6.9 %collective-permute-start.19 = (bf16[128,128]{1,0:T(8,128)(2,1)S(1)}, bf16[128,128]{1,0:T(8,128)(2,1)S(1)}, u32[]{:S(2)}, u32[]{:S(2)}) collective-permute-start(bf16[128,128]{1,0:T(8,128)(2,1)S(1)} %get-tuple-element.73), channel_id=1, source_target_pairs={{0,1},{1,2},{2,3},{3,0},{4,5},{5,6},{6,7},{7,4},{8,9},{9,10},{10,1... | collective-permute-start | bytes 98312 | tf_op jit(solution)/shard_map/ppermute | solution.py:406
  181.8 12.1 %collective-permute-start.14 = (bf16[8,80,128]{2,1,0:T(8,128)(2,1)S(1)}, bf16[8,80,128]{2,1,0:T(8,128)(2,1)S(1)}, u32[]{:S(2)}, u32[]{:S(2)}) collective-permute-start(bf16[8,80,128]{2,1,0:T(8,128)(2,1)S(1)} %get-tuple-element.62), channel_id=1, source_target_pairs={{0,8},{4,12},{8,16},{12,20},{16,24},{20,28},{24,0},{28,4},{32,40},... | collective-permute-start | bytes 491528 | tf_op jit(solution)/shard_map/ppermute | solution.py:398
  183.3 15.8 %collective-permute-start.15 = (bf16[8,80,128]{2,1,0:T(8,128)(2,1)S(1)}, bf16[8,80,128]{2,1,0:T(8,128)(2,1)S(1)}, u32[]{:S(2)}, u32[]{:S(2)}) collective-permute-start(bf16[8,80,128]{2,1,0:T(8,128)(2,1)S(1)} %get-tuple-element.64), channel_id=1, source_target_pairs={{0,16},{4,20},{8,24},{12,28},{16,0},{20,4},{24,8},{28,12},{32,48},... | collective-permute-start | bytes 491528 | tf_op jit(solution)/shard_map/ppermute | solution.py:398
  186.0 13.1 %collective-permute-start.16 = (bf16[8,80,128]{2,1,0:T(8,128)(2,1)S(1)}, bf16[8,80,128]{2,1,0:T(8,128)(2,1)S(1)}, u32[]{:S(2)}, u32[]{:S(2)}) collective-permute-start(bf16[8,80,128]{2,1,0:T(8,128)(2,1)S(1)} %get-tuple-element.63), channel_id=1, source_target_pairs={{0,24},{4,28},{8,0},{12,4},{16,8},{20,12},{24,16},{28,20},{32,56},... | collective-permute-start | bytes 491528 | tf_op jit(solution)/shard_map/ppermute | solution.py:398
  216.0 7.8 %collective-permute-start.22 = (bf16[1,80,128]{2,1,0:T(8,128)(2,1)S(1)}, bf16[1,80,128]{2,1,0:T(8,128)(2,1)S(1)}, u32[]{:S(2)}, u32[]{:S(2)}) collective-permute-start(bf16[1,80,128]{2,1,0:T(8,128)(2,1)S(1)} %constant_dynamic-slice_fusion), channel_id=1, source_target_pairs={{0,128},{4,132},{8,136},{12,140},{16,144},{20,148},{24,152},{28,15... | collective-permute-start | bytes 61448 | tf_op jit(solution)/shard_map/ppermute | solution.py:505
  223.8 6.9 %collective-permute-start.23 = (f32[80,128]{1,0:T(8,128)S(1)}, f32[80,128]{1,0:T(8,128)S(1)}, u32[]{:S(2)}, u32[]{:S(2)}) collective-permute-start(f32[80,128]{1,0:T(8,128)S(1)} %multiply_bitcast_fusion), channel_id=1, source_target_pairs={{0,3},{1,0},{2,1},{3,2},{4,7},{5,4},{6,5},{7,6},{8,11},{9,8},{10,9... | collective-permute-start | bytes 122888 | tf_op jit(solution)/shard_map/ppermute | solution.py:406
  (24 other events, 170.7 us)
Sparse Core Ops, SparseCore 0:
  9.8 89.2 all-gather.2
  105.3 63.5 all-gather.4
where the time goes:
time: 241 us; the launch traced here: 240 us
  waiting for transfers between devices  92.7 us (38%)
  starting transfers between devices  68.5 us (28%)
  Pallas kernels  51.2 us (21%)
  between operations  14.4 us (6%)
  local copies, waits for them, and re-layouts  10 us (4%)
  other arithmetic  3.58 us (1%)
    all_gather x1, waiting for transfers between devices, shards(): x_all = lax.all_gather(x_saved, 'seq', axis=0, tiled=True)  32.6 us
    ppermute x6, waiting for transfers between devices, along_x(): lax.ppermute(value, 'dp', [(dp_of(z, x, c), dp_of(z, (x + d) % NX, c)) fo...  23 us
    ppermute x9, starting transfers between devices, along_seq(): return lax.ppermute(value, 'seq', [(s, (s + d) % NS) for s in range(NS)])  13.1 us
    all_to_all x1, starting transfers between devices, shards(): lax.all_to_all(rows.reshape(NDP * NS, 48, HEAD), ('dp', 'seq'), split_axi...  12.1 us
    ppermute x6, starting transfers between devices, along_x(): lax.ppermute(value, 'dp', [(dp_of(z, x, c), dp_of(z, (x + d) % NX, c)) fo...  11.1 us
    all_to_all x1, waiting for transfers between devices, shards(): lax.all_to_all(rows.reshape(NDP * NS, 48, HEAD), ('dp', 'seq'), split_axi...  11 us
    ppermute x3, starting transfers between devices, shards(): other = lax.ppermute(stage, 'dp', swap)  9.79 us
    ppermute x3, waiting for transfers between devices, shards(): total = keep.astype(F32) + lax.ppermute(give, 'dp', swap).astype(F32)  8.91 us
  transfers between devices with their start and end apart: 31, of which 16 were waited for; matrix products, arithmetic and copies ran while one was open for 4% of the time, Pallas kernels for 21%

commit v1 on v0

v1 whole, which is shorter than its diff:
```python
import functools
import math

import jax
import jax.numpy as jnp
from jax import lax
from jax.experimental import pallas as pl
from jax.experimental.pallas import tpu as pltpu
from jax.sharding import PartitionSpec as P

HEAD = 128
CAP = 4
NZ, NX, NC, NS = 8, 4, 2, 4
NDP = NZ * NX * NC
ROWS = 128
GROUP = ROWS * NS
PER = 5
QW = PER * HEAD
BF = jnp.bfloat16
F32 = jnp.float32
SCALE = HEAD ** (-0.5)
LIMIT = 58 * 1024 * 1024
SMALL = 24 * 1024 * 1024
BIG = 62 * 1024 * 1024

VMEM = pl.BlockSpec(memory_space=pltpu.VMEM)
SMEM = pl.BlockSpec(memory_space=pltpu.SMEM)
HBM = pl.BlockSpec(memory_space=pltpu.HBM)


def params(limit=LIMIT):
    return pltpu.CompilerParams(vmem_limit_bytes=limit)


def cost(flops, bytes_accessed):
    return pl.CostEstimate(flops=int(flops), bytes_accessed=int(bytes_accessed), transcendentals=0)


def ones_where(hit):
    return jnp.where(hit, 1.0, 0.0).astype(BF)


def mm(a, b):
    return jnp.dot(a, b, preferred_element_type=F32)


def mm_nt(a, b):
    return lax.dot_general(a, b, (((1,), (1,)), ((), ())), preferred_element_type=F32)


def mm_tn(a, b):
    return lax.dot_general(a, b, (((0,), (0,)), ((), ())), preferred_element_type=F32)


def column(row):
    n = row.shape[1]
    at = lax.broadcasted_iota(jnp.int32, (n, n), 0) == lax.broadcasted_iota(jnp.int32, (n, n), 1)
    return jnp.sum(jnp.where(at, row.astype(F32), 0.0), axis=1, keepdims=True)


def slot_column(row):
    return column(row).astype(jnp.int32)


def pack_rows_kernel(slots_ref, coef_ref, q_ref, k_ref, g_ref, out_ref):
    coef = column(coef_ref[...])
    row = lax.broadcasted_iota(jnp.int32, (256, 1), 0)
    wanted = (pl.program_id(0) * 16 + row // 16) * CAP + row % 4
    place = (row % 16) // 4
    own = slots_ref[...]
    onehot = jnp.concatenate(
        [ones_where(jnp.where(place == m, wanted, -1) == own) for m in range(4)], axis=1
    )

    def chunk(s, m):
        if m < PER:
            return q_ref[:, s * QW + m * HEAD : s * QW + (m + 1) * HEAD]
        if m < 2 * PER + 1 and m > PER:
            at = s * QW + (m - PER - 1) * HEAD
            return (coef * g_ref[:, at : at + HEAD].astype(F32)).astype(BF)
        return k_ref[:, s * HEAD : (s + 1) * HEAD]

    for t in range(3):
        rhs = jnp.concatenate(
            [
                jnp.concatenate([chunk(s, 4 * t + m) for m in range(4)], axis=0)
                for s in range(NS)
            ],
            axis=1,
        )
        res = mm(onehot, rhs).astype(BF)
        for s in range(NS):
            out_ref[:, s, 16 * t : 16 * t + 16, :] = res[:, s * HEAD : (s + 1) * HEAD].reshape(
                16, 16, HEAD
            )


def pack_rows(slots, coef, q, k, g):
    return pl.pallas_call(
        pack_rows_kernel,
        grid=(4,),
        out_shape=jax.ShapeDtypeStruct((NDP, NS, 48, HEAD), BF),
        in_specs=[
            pl.BlockSpec((1, ROWS), lambda i: (0, 0)),
            pl.BlockSpec((1, ROWS), lambda i: (0, 0)),
            pl.BlockSpec((ROWS, NS * QW), lambda i: (0, 0)),
            pl.BlockSpec((ROWS, NS * HEAD), lambda i: (0, 0)),
            pl.BlockSpec((ROWS, NS * QW), lambda i: (0, 0)),
        ],
        out_specs=pl.BlockSpec((16, NS, 48, HEAD), lambda i: (i, 0, 0, 0)),
        compiler_params=params(SMALL),
        cost_estimate=cost(1.6e9, 5e6),
        name="pack_rows",
    )(slots, coef, q, k, g)


def values_kernel(place_ref, slot_ref, x_ref, *refs):
    pieces, (out_ref, w_ref) = refs[: NX * NC], refs[NX * NC :]
    block = w_ref.shape[0] // NDP
    for dx in range(NX):
        for dc in range(NC):
            at = lax.rem(place_ref[0] - dx + NX, NX) * NC + lax.rem(place_ref[1] + dc, NC)
            for held in range(NZ):
                at_z = (held % 2) * 4 + jnp.bitwise_xor(place_ref[2] % 4, held // 2)
                start = pl.multiple_of((at_z * NX * NC + at) * block, 16)
                w_ref[pl.ds(start, block), :] = pieces[dx * NC + dc][held]
    row = lax.broadcasted_iota(jnp.int32, (NDP * 16, 1), 0)
    wanted = (row // 16) * CAP + row % 4
    of_seq = (row % 16) // 4
    value = mm(x_ref[...], w_ref[...]).astype(BF)
    spread = jnp.concatenate(
        [
            ones_where(jnp.where(of_seq == s, wanted, -1) == slot_ref[s : s + 1, :])
            for s in range(NS)
        ],
        axis=1,
    )
    out_ref[...] = mm(spread, value).astype(BF).reshape(NDP, 16, HEAD)


def values_of(place, slots, x_all, pieces):
    depth = x_all.shape[1]
    return pl.pallas_call(
        values_kernel,
        out_shape=(
            jax.ShapeDtypeStruct((NDP, 16, HEAD), BF),
            jax.ShapeDtypeStruct((depth, HEAD), BF),
        ),
        in_specs=[SMEM] + [VMEM] * (2 + NX * NC),
        out_specs=(VMEM, VMEM),
        compiler_params=params(BIG),
        cost_estimate=cost(0.8e9, 8e6),
        name="values",
    )(place, slots, x_all, *pieces)


def turn_kernel(x_ref, out_ref):
    out_ref[...] = x_ref[...].T


def turn(x_all):
    depth = x_all.shape[1]
    width = depth // NZ
    return pl.pallas_call(
        turn_kernel,
        grid=(NZ,),
        out_shape=jax.ShapeDtypeStruct((depth, GROUP), BF),
        in_specs=[pl.BlockSpec((GROUP, width), lambda i: (0, i))],
        out_specs=pl.BlockSpec((width, GROUP), lambda i: (i, 0)),
        compiler_params=params(),
        cost_estimate=cost(1e6, 11e6),
        name="turn",
    )(x_all)


def window(s):
    return max(0, s - 2) * ROWS, (s + 1) * ROWS


def probs_kernel(len_ref, slot_ref, r_ref, v_ref, *refs):
    outs, (both, qs, ks, ds, p0, p1, p2, p3, dv, sems) = refs[:8], refs[8:]
    both_out, qs_out, ks_out, ds_out = outs[:4]
    copies = []

    def send(src, dst):
        copy = pltpu.make_async_copy(src, dst, sems.at[len(copies)])
        copy.start()
        copies.append(copy)

    both[:, 0:16, :] = v_ref[...]
    lane = lax.broadcasted_iota(jnp.int32, (1, NDP * 16), 1)
    wanted = (lane // 16) * CAP + lane % 4
    place = (lane % 16) // 4
    for s in range(NS):
        own = slot_column(slot_ref[s : s + 1, :])
        pick = jnp.concatenate(
            [ones_where(jnp.where(place == m, wanted, -1) == own) for m in range(4)], axis=0
        )
        rhs = jnp.concatenate(
            [r_ref[:, s, 16 * t : 16 * t + 16, :].reshape(NDP * 16, HEAD) for t in range(3)],
            axis=1,
        )
        res = mm(pick, rhs).astype(BF)
        qs[s, 0:512, :] = res[:, 0:128]
        qs[s, 512:640, :] = res[0:128, 128:256]
        ks[s * ROWS : (s + 1) * ROWS, :] = res[128:256, 128:256]
        ds[s, 0:256, :] = res[256:512, 128:256]
        ds[s, 256:640, :] = res[0:384, 256:384]
        send(qs.at[s], qs_out.at[s])
        send(ds.at[s], ds_out.at[s])
    send(ks, ks_out)

    first, second = len_ref[0], len_ref[0] + len_ref[1]
    dv[...] = jnp.zeros_like(dv)
    for s, p_ref in enumerate((p0, p1, p2, p3)):
        lo, hi = window(s)
        width = hi - lo
        q_pos = s * ROWS + lax.broadcasted_iota(jnp.int32, (ROWS, width), 0)
        k_pos = lo + lax.broadcasted_iota(jnp.int32, (ROWS, width), 1)
        begin = jnp.where(q_pos >= second, second, jnp.where(q_pos >= first, first, 0))
        visible = (k_pos <= q_pos) & (k_pos >= begin)
        scores = mm_nt(qs[s], ks[lo:hi, :]).reshape(PER, ROWS, width) * SCALE
        scores = jnp.where(visible[None], scores, -jnp.inf)
        weights = jnp.exp(scores - jnp.max(scores, axis=2, keepdims=True))
        probs = weights / jnp.sum(weights, axis=2, keepdims=True)
        half = probs.astype(BF).reshape(PER * ROWS, width)
        p_ref[...] = half
        send(p_ref, outs[4 + s])
        dv[lo:hi, :] += mm_tn(half, ds[s])

    row = lax.broadcasted_iota(jnp.int32, (NDP * 16, 1), 0)
    wanted = (row // 16) * CAP + row % 4
    of_seq = (row % 16) // 4
    spread = jnp.concatenate(
        [
            ones_where(jnp.where(of_seq == s, wanted, -1) == slot_ref[s : s + 1, :])
            for s in range(NS)
        ],
        axis=1,
    )
    both[:, 16:32, :] = mm(spread, dv[...].astype(BF)).astype(BF).reshape(NDP, 16, HEAD)
    send(both, both_out)
    for copy in copies:
        copy.wait()


def probs_of(lengths, slots, r, v):
    shapes = [
        (NDP, 32, HEAD),
        (NS, PER * ROWS, HEAD),
        (GROUP, HEAD),
        (NS, PER * ROWS, HEAD),
    ] + [(PER * ROWS, window(s)[1] - window(s)[0]) for s in range(NS)]
    return pl.pallas_call(
        probs_kernel,
        out_shape=tuple(jax.ShapeDtypeStruct(shape, BF) for shape in shapes),
        in_specs=[SMEM, VMEM, VMEM, VMEM],
        out_specs=(HBM,) * len(shapes),
        scratch_shapes=[pltpu.VMEM(shape, BF) for shape in shapes]
        + [pltpu.VMEM((GROUP, HEAD), F32), pltpu.SemaphoreType.DMA((3 * NS + 2,))],
        compiler_params=params(BIG),
        cost_estimate=cost(3e9, 9e6),
        name="probs",
    )(lengths, slots, r, v)


def grads_kernel(slot_ref, r_ref, *refs):
    kept, dqk_out, held = refs[:7], refs[7], refs[8:15]
    qs, ks, ds = held[:3]
    out, vs, dq, dk, in_sems, out_sems = refs[15:]
    arrivals = [
        pltpu.make_async_copy(kept[n], held[n], in_sems.at[n]) for n in (2, 1, 0, 3, 4, 5, 6)
    ]
    for copy in arrivals:
        copy.start()
    lane = lax.broadcasted_iota(jnp.int32, (1, NDP * 16), 1)
    wanted = (lane // 16) * CAP + lane % 4
    of_seq = (lane % 16) // 4
    pick = jnp.concatenate(
        [
            ones_where(jnp.where(of_seq == s, wanted, -1) == slot_column(slot_ref[s : s + 1, :]))
            for s in range(NS)
        ],
        axis=0,
    )
    vs[...] = mm(pick, r_ref[:, 0:16, :].reshape(NDP * 16, HEAD)).astype(BF)
    dk[...] = jnp.zeros_like(dk)
    for copy in arrivals:
        copy.wait()
    for s in range(NS):
        lo, hi = window(s)
        probs = held[3 + s][...].astype(F32)
        dprobs = mm_nt(ds[s], vs[lo:hi, :])
        delta = jnp.sum(probs * dprobs, axis=1, keepdims=True)
        dscores = (probs * (dprobs - delta)).astype(BF)
        dq[s] = (mm(dscores, ks[lo:hi, :]) * SCALE).astype(BF)
        dk[lo:hi, :] += mm_tn(dscores, qs[s])

    row = lax.broadcasted_iota(jnp.int32, (NDP * 8, 1), 0)
    wanted = (row // 8) * CAP + row % 4
    place = (row % 8) // 4
    for s in range(NS):
        own = slot_ref[s : s + 1, :]
        spread = jnp.concatenate(
            [ones_where(jnp.where(place == m, wanted, -1) == own) for m in range(2)], axis=1
        )
        own_k = (dk[s * ROWS : (s + 1) * ROWS, :] * SCALE).astype(BF)
        rhs = jnp.concatenate(
            [
                dq[s, 0:256, :],
                dq[s, 256:512, :],
                jnp.concatenate([dq[s, 512:640, :], own_k], axis=0),
            ],
            axis=1,
        )
        res = mm(spread, rhs)
        for t in range(3):
            out[s, :, 8 * t : 8 * t + 8, :] = (
                res[:, t * HEAD : (t + 1) * HEAD].reshape(NDP, 8, HEAD).astype(BF)
            )
        pltpu.make_async_copy(out.at[s], dqk_out.at[:, s], out_sems.at[s]).start()
    for s in range(NS):
        pltpu.make_async_copy(out.at[s], dqk_out.at[:, s], out_sems.at[s]).wait()


def grads_of(slots, r, kept):
    return pl.pallas_call(
        grads_kernel,
        out_shape=jax.ShapeDtypeStruct((NDP, NS, 24, HEAD), BF),
        in_specs=[VMEM] * 2 + [HBM] * len(kept),
        out_specs=HBM,
        scratch_shapes=[pltpu.VMEM(one.shape, BF) for one in kept]
        + [
            pltpu.VMEM((NS, NDP, 24, HEAD), BF),
            pltpu.VMEM((GROUP, HEAD), BF),
            pltpu.VMEM((NS, PER * ROWS, HEAD), BF),
            pltpu.VMEM((GROUP, HEAD), F32),
            pltpu.SemaphoreType.DMA((len(kept),)),
            pltpu.SemaphoreType.DMA((NS,)),
        ],
        compiler_params=params(SMALL),
        cost_estimate=cost(3e9, 8e6),
        name="grads",
    )(slots, r, *kept)


def weight_terms_kernel(slot_ref, r_ref, x_ref, dv_ref, out_ref):
    @pl.when(pl.program_id(0) == 0)
    def _():
        lane = lax.broadcasted_iota(jnp.int32, (1, NDP * 16), 1)
        wanted = (lane // 16) * CAP + lane % 4
        of_seq = (lane % 16) // 4
        pick = []
        for s in range(NS):
            own = slot_column(slot_ref[s : s + 1, :])
            pick.append(ones_where(jnp.where(of_seq == s, wanted, -1) == own))
        rows = r_ref[...].reshape(NDP * 16, HEAD)
        dv_ref[...] = mm(jnp.concatenate(pick, axis=0), rows).astype(BF)

    terms = mm(x_ref[...], dv_ref[...]).astype(BF)
    block = out_ref.shape[3]
    for z in range(out_ref.shape[2]):
        for x in range(NX):
            for c in range(NC):
                at = ((z * NX + x) * NC + c) * block
                out_ref[c, x, z] = terms[at : at + block, :]


def weight_terms(slots, r, x_turned):
    block = x_turned.shape[0] // NDP
    steps = 4
    each = NZ // steps
    return pl.pallas_call(
        weight_terms_kernel,
        grid=(steps,),
        out_shape=(
            jax.ShapeDtypeStruct((GROUP, HEAD), BF),
            jax.ShapeDtypeStruct((NC, NX, NZ, block, HEAD), BF),
        ),
        in_specs=[
            pl.BlockSpec((NS, ROWS), lambda i: (0, 0)),
            pl.BlockSpec((NDP, 16, HEAD), lambda i: (0, 1, 0)),
            pl.BlockSpec((each * NX * NC * block, GROUP), lambda i: (i, 0)),
        ],
        out_specs=(
            pl.BlockSpec((GROUP, HEAD), lambda i: (0, 0)),
            pl.BlockSpec((NC, NX, each, block, HEAD), lambda i: (0, 0, i, 0, 0)),
        ),
        compiler_params=params(),
        cost_estimate=cost(0.8e9, 7e6),
        name="weight_terms",
    )(slots, r, x_turned)


def grad_x_kernel(dv_ref, w_ref, out_ref):
    dv = jnp.concatenate([dv_ref[s] for s in range(NS)], axis=1)
    w = jnp.concatenate([w_ref[s] for s in range(NS)], axis=1)
    out_ref[...] = mm_nt(dv, w).astype(BF)


def grad_x_of(dv, w):
    depth = w.shape[1]
    width = 1024
    return pl.pallas_call(
        grad_x_kernel,
        grid=(depth // width,),
        out_shape=jax.ShapeDtypeStruct((ROWS, depth), BF),
        in_specs=[
            pl.BlockSpec((NS, ROWS, HEAD), lambda i: (0, 0, 0)),
            pl.BlockSpec((NS, width, HEAD), lambda i: (0, i, 0)),
        ],
        out_specs=pl.BlockSpec((ROWS, width), lambda i: (0, i)),
        compiler_params=params(),
        cost_estimate=cost(0.7e9, 7e6),
        name="grad_x",
    )(dv, w)


def unpack_kernel(slot_ref, r_ref, q_ref, k_ref):
    lane = lax.broadcasted_iota(jnp.int32, (1, NDP * 8), 1)
    wanted = (lane // 8) * CAP + lane % 4
    place = (lane % 8) // 4
    own = slot_column(slot_ref[...])
    pick = jnp.concatenate(
        [ones_where(jnp.where(place == m, wanted, -1) == own) for m in range(2)], axis=0
    )
    for s in range(NS):
        rhs = jnp.concatenate(
            [
                r_ref[:, s, 8 * t : 8 * t + 8, :].astype(F32).reshape(NDP * 8, HEAD).astype(BF)
                for t in range(3)
            ],
            axis=1,
        )
        res = mm(pick, rhs).astype(BF)
        for m in range(PER):
            t, at = m // 2, (m % 2) * ROWS
            q_ref[:, s * QW + m * HEAD : s * QW + (m + 1) * HEAD] = res[
                at : at + ROWS, t * HEAD : (t + 1) * HEAD
            ]
        k_ref[:, s * HEAD : (s + 1) * HEAD] = res[ROWS : 2 * ROWS, 2 * HEAD : 3 * HEAD]


def unpack(slots, r):
    return pl.pallas_call(
        unpack_kernel,
        out_shape=(
            jax.ShapeDtypeStruct((ROWS, NS * QW), BF),
            jax.ShapeDtypeStruct((ROWS, NS * HEAD), BF),
        ),
        in_specs=[VMEM, VMEM],
        out_specs=(VMEM, VMEM),
        compiler_params=params(),
        cost_estimate=cost(0.5e9, 4e6),
        name="unpack",
    )(slots, r)


def dp_of(z, x, c):
    return (z * NX + x) * NC + c


EACH = [(z, x, c) for z in range(NZ) for x in range(NX) for c in range(NC)]


def along_z(value, d):
    return lax.ppermute(value, "dp", [(dp_of(z, x, c), dp_of((z + d) % NZ, x, c)) for z, x, c in EACH])


def along_x(value, d):
    return lax.ppermute(value, "dp", [(dp_of(z, x, c), dp_of(z, (x + d) % NX, c)) for z, x, c in EACH])


def along_c(value):
    return lax.ppermute(value, "dp", [(dp_of(z, x, c), dp_of(z, x, 1 - c)) for z, x, c in EACH])


def along_seq(value, d):
    return lax.ppermute(value, "seq", [(s, (s + d) % NS) for s in range(NS)])


def rank_of(label, key):
    same = (label[:, None] == label[None, :]) & (key[None, :] < key[:, None])
    return jnp.sum(same.astype(jnp.int32), axis=1)


def in_order(parts, own):
    count = len(parts)
    index = jnp.arange(count, dtype=jnp.int32).reshape((count,) + (1,) * parts[0].ndim)
    total = jnp.zeros((count,) + parts[0].shape, parts[0].dtype)
    for d, part in enumerate(parts):
        total = jnp.where(index == (own - d) % count, part[None], total)
    return total


def shards(
    x_saved, q_saved, k_saved, grad_attn, token_coef, dest_of, source_of, lengths, value_weight
):
    dp, seq = lax.axis_index("dp"), lax.axis_index("seq")
    z, x, c = dp // (NX * NC), (dp // NC) % NX, dp % NC

    def pick(value, at):
        return lax.dynamic_index_in_dim(value, at, 0, keepdims=False)

    target = dest_of // GROUP
    send_slot = target * CAP + rank_of(target, jnp.arange(ROWS, dtype=jnp.int32))
    anchor = source_of // GROUP
    recv_slot = anchor * CAP + rank_of(anchor, source_of)
    slots = jnp.stack([send_slot, recv_slot])

    def across_z(value, bits):
        swap = [(dp_of(a, b, e), dp_of(a ^ bits, b, e)) for a, b, e in EACH]
        return lax.ppermute(value, "dp", swap)

    own_w = lax.dynamic_slice_in_dim(value_weight, seq * HEAD, HEAD, axis=1)
    far_w = across_z(own_w, 4)
    low = z < 4
    stage = jnp.stack([jnp.where(low, own_w, far_w), jnp.where(low, far_w, own_w)])
    stage = jnp.concatenate([stage] + [across_z(stage, bits) for bits in (1, 2, 3)], axis=0)

    own_slot = send_slot[None]
    rows = pack_rows(own_slot, token_coef[None], q_saved, k_saved, grad_attn)
    rows, slots, stage = lax.optimization_barrier((rows, slots, stage))
    arrived = lax.all_to_all(
        rows.reshape(NDP * NS, 48, HEAD), ("dp", "seq"), split_axis=0, concat_axis=0, tiled=True
    )

    all_slots = in_order([slots] + [along_seq(slots, d) for d in range(1, NS)], seq)
    send_all, recv_all = all_slots[:, 0], all_slots[:, 1]
    x_all = lax.all_gather(x_saved, "seq", axis=0, tiled=True)

    pieces = []
    for part in [stage] + [along_x(stage, d) for d in range(1, NX)]:
        pieces += [part, along_c(part)]
    place = jnp.stack([x, c, z]).astype(jnp.int32)
    v_out, head_w = values_of(place, send_all, x_all, pieces)
    w_all = lax.all_gather(head_w, "seq", axis=0, tiled=True)

    arrived, recv_all, v_out = lax.optimization_barrier((arrived, recv_all, v_out))
    both, *kept = probs_of(lengths[0], recv_all, arrived.reshape(NDP, NS, 48, HEAD), v_out)
    both = lax.all_to_all(both, "dp", split_axis=0, concat_axis=0, tiled=True)
    x_turned = turn(x_all)
    both, x_turned = lax.optimization_barrier((both, x_turned))
    dqk_out = grads_of(recv_all, both, kept)
    dqk_out, send_all = lax.optimization_barrier((dqk_out, send_all))
    dv_head, terms = weight_terms(send_all, both, x_turned)

    dqk_back = lax.all_to_all(
        dqk_out.reshape(NDP * NS, 24, HEAD), ("dp", "seq"), split_axis=0, concat_axis=0, tiled=True
    )

    part = pick(terms, c).astype(F32) + along_c(pick(terms, 1 - c)).astype(F32)
    part = part.astype(BF)
    total = pick(part, x).astype(F32)
    for d in range(1, NX):
        total = total + along_x(pick(part, (x + d) % NX), d).astype(F32)
    dv_view = dv_head.reshape(NS, ROWS, HEAD)
    dv_parts = [pick(dv_view, seq)]
    for d in range(1, NS):
        dv_parts.append(along_seq(pick(dv_view, (seq + d) % NS), d))
    grad_x = grad_x_of(in_order(dv_parts, seq), w_all.reshape(NS, -1, HEAD))

    total, grad_x, dqk_back = lax.optimization_barrier((total, grad_x, dqk_back))
    half = total.astype(BF).reshape(NZ // 2, 2, *total.shape[1:])
    keep = lax.dynamic_index_in_dim(half, z % 2, 1, keepdims=False)
    give = lax.dynamic_index_in_dim(half, 1 - z % 2, 1, keepdims=False)
    half = (keep.astype(F32) + across_z(give, 1).astype(F32)).astype(BF)
    total = pick(half, z // 2).astype(F32)
    for bits in (1, 2, 3):
        total = total + across_z(pick(half, (z // 2) ^ bits), 2 * bits).astype(F32)
    own = total / math.sqrt(GROUP * NDP)
    heads = in_order([own] + [along_seq(own, d) for d in range(1, NS)], seq)
    grad_v_weight = jnp.concatenate([heads[s] for s in range(NS)], axis=1)

    grad_q, grad_k = unpack(own_slot, dqk_back.reshape(NDP, NS, 24, HEAD))
    return (grad_x, grad_q, grad_k, grad_v_weight)


def solution(mesh):
    rows = P(("dp", "seq"), None)
    flat = P(("dp", "seq"))
    whole = P("dp", None)
    return jax.shard_map(
        shards,
        mesh=mesh,
        in_specs=(rows, rows, rows, rows, flat, flat, flat, whole, whole),
        out_specs=(rows, rows, rows, whole),
        check_vma=False,
    )
```

time: 241 us -> 232 us (0.963)
  local copies, waits for them, and re-layouts: 10 us -> 5.31 us
  Pallas kernels: 51.2 us -> 46.6 us
    all_to_all x1, waiting for transfers between devices: 0.9 us -> 4.88 us  [shards(): lax.all_to_all(dqk_out.reshape(NDP * NS, 24, HEAD), ('dp', 'seq'), split_...]
    all_to_all x1, waiting for transfers between devices: 11 us -> 7.69 us  [shards(): lax.all_to_all(rows.reshape(NDP * NS, 48, HEAD), ('dp', 'seq'), split_axi...]
    all_gather x1, waiting for transfers between devices: 32.6 us -> 35.4 us  [shards(): x_all = lax.all_gather(x_saved, 'seq', axis=0, tiled=True)]
    optimization_barrier x3 -> x0, local copies, waits for them, and re-layouts: 2.58 us -> none  [the longest x2 1.72 us: shards(): lax.optimization_barrier((arrived, send_col, recv_col, own_col, v_out))]
    ppermute x6 -> x8, waiting for transfers between devices: 13.5 us -> 11.6 us  [across_z(): return lax.ppermute(value, 'dp', swap)]
    ppermute x6 -> x8, starting transfers between devices: 17.5 us -> 17.1 us  [across_z(): return lax.ppermute(value, 'dp', swap)]
  transfers between devices with their start and end apart: 31 -> 33, of which waited for: 16 -> 20; matrix products, arithmetic and copies ran while one was open for 4% -> 3% of each run, Pallas kernels for 21% -> 20%
where the time goes in v1:
time: 232 us; the launch traced here: 231 us
  waiting for transfers between devices  94.1 us (41%)
  starting transfers between devices  67.9 us (29%)
  Pallas kernels  46.6 us (20%)
  between operations  14.6 us (6%)
  local copies, waits for them, and re-layouts  5.31 us (2%)
  other arithmetic  2.95 us (1%)
    all_gather x1, waiting for transfers between devices, shards(): x_all = lax.all_gather(x_saved, 'seq', axis=0, tiled=True)  35.4 us
    ppermute x6, waiting for transfers between devices, along_x(): lax.ppermute(value, 'dp', [(dp_of(z, x, c), dp_of(z, (x + d) % NX, c)) fo...  21.3 us
    ppermute x8, starting transfers between devices, across_z(): return lax.ppermute(value, 'dp', swap)  17.1 us
    all_to_all x1, starting transfers between devices, shards(): lax.all_to_all(rows.reshape(NDP * NS, 48, HEAD), ('dp', 'seq'), split_axi...  13.2 us
    ppermute x9, starting transfers between devices, along_seq(): return lax.ppermute(value, 'seq', [(s, (s + d) % NS) for s in range(NS)])  11.8 us
    ppermute x8, waiting for transfers between devices, across_z(): return lax.ppermute(value, 'dp', swap)  11.6 us
    ppermute x6, starting transfers between devices, along_x(): lax.ppermute(value, 'dp', [(dp_of(z, x, c), dp_of(z, (x + d) % NX, c)) fo...  10.7 us
    all_to_all x1, waiting for transfers between devices, shards(): both = lax.all_to_all(both, 'dp', split_axis=0, concat_axis=0, tiled=True)  8.66 us
  transfers between devices with their start and end apart: 33, of which 20 were waited for; matrix products, arithmetic and copies ran while one was open for 3% of the time, Pallas kernels for 20%

profile of v1, /device:TPU:32, one launch (start us, length us, event | category | flops | bytes accessed | tf_op | source)
XLA Modules:
  0.0 231.4 jit_solution(17783971656033725396)
XLA Ops:
  8.7 6.3 %collective-permute-start = (bf16[80,128]{1,0:T(8,128)(2,1)S(1)}, bf16[80,128]{1,0:T(8,128)(2,1)S(1)}, u32[]{:S(2)}, u32[]{:S(2)}) collective-permute-start(bf16[80,128]{1,0:T(8,128)(2,1)S(1)} %constant_dynamic-slice_fusion), channel_id=1, source_target_pairs={{0,128},{4,132},{8,136},{12,140},{16,144},{20,148},{24,152},{28,15... | collective-permute-start | bytes 61448 | tf_op jit(solution)/shard_map/ppermute | solution.py:513
  16.3 3.6 %pack_rows.1 = bf16[64,4,48,128]{3,2,1,0:T(8,128)(2,1)} custom-call(s32[1,128]{1,0:T(1,128)S(1)} %add_bitcast_fusion.1.slots_ref.slot_ref, f32[1,128]{1,0:T(1,128)S(1)} %bitcast.70, bf16[128,2560]{1,0:T(8,128)(2,1)S(1)} %copy-done.3, bf16[128,512]{1,0:T(8,128)(2,1)S(1)} %copy-done.5, bf16[128,2560]{1,0:T(8,128)(2,1)S(1)} %copy-done.4), custom_call_target="tpu_custom_call" | custom-call | flops 1600000000 | bytes 5000000 | tf_op jit(solution)/shard_map/pack_rows/pallas_call | solution.py:99
  27.0 13.2 %all-to-all-start = ((bf16[256,48,128]{2,1,0:T(8,128)(2,1)}), bf16[256,48,128]{2,1,0:T(8,128)(2,1)}, u32[]{:S(2)}, u32[]{:S(2)}) async-start(bf16[256,48,128]{2,1,0:T(8,128)(2,1)} %bitcast.5), calls=%async_computation | async-start | bytes 6291456 | tf_op jit(solution)/shard_map/all_to_all | solution.py:524
  40.4 3.0 %collective-permute-start.4 = (s32[2,128]{1,0:T(2,128)S(1)}, s32[2,128]{1,0:T(2,128)S(1)}, u32[]{:S(2)}, u32[]{:S(2)}) collective-permute-start(s32[2,128]{1,0:T(2,128)S(1)} %pad_add_fusion), channel_id=1, source_target_pairs={{0,3},{1,0},{2,1},{3,2},{4,7},{5,4},{6,5},{7,6},{8,11},{9,8},{10,9... | collective-permute-start | bytes 3080 | tf_op jit(solution)/shard_map/ppermute | solution.py:479
  45.6 3.0 %collective-permute-start.10 = (bf16[8,80,128]{2,1,0:T(8,128)(2,1)S(1)}, bf16[8,80,128]{2,1,0:T(8,128)(2,1)S(1)}, u32[]{:S(2)}, u32[]{:S(2)}) collective-permute-start(bf16[8,80,128]{2,1,0:T(8,128)(2,1)S(1)} %constant_dynamic-update-slice_fusion.refs_0_), channel_id=1, source_target_pairs={{0,16},{4,20},{8,24},{12,28},{16,0},{20,4},{24,8},{28,12},{32,48},... | collective-permute-start | bytes 491528 | tf_op jit(solution)/shard_map/ppermute | solution.py:471
  51.9 4.4 %collective-permute-done.10.refs_4_ = bf16[8,80,128]{2,1,0:T(8,128)(2,1)S(1)} collective-permute-done((bf16[8,80,128]{2,1,0:T(8,128)(2,1)S(1)}, bf16[8,80,128]{2,1,0:T(8,128)(2,1)S(1)}, u32[]{:S(2)}, u32[]{:S(2)}) %collective-permute-start.10) | collective-permute-done | bytes 163872 | tf_op jit(solution)/shard_map/ppermute | solution.py:471
  56.2 7.1 %collective-permute-done.12.refs_6_ = bf16[8,80,128]{2,1,0:T(8,128)(2,1)S(1)} collective-permute-done((bf16[8,80,128]{2,1,0:T(8,128)(2,1)S(1)}, bf16[8,80,128]{2,1,0:T(8,128)(2,1)S(1)}, u32[]{:S(2)}, u32[]{:S(2)}) %collective-permute-start.12) | collective-permute-done | bytes 163872 | tf_op jit(solution)/shard_map/ppermute | solution.py:471
  65.0 35.4 %all-gather.3.cloned.1.call-done.x_ref = bf16[512,5120]{1,0:T(8,128)(2,1)} async-done(((bf16[128,5120]{1,0:T(8,128)(2,1)}), bf16[512,5120]{1,0:T(8,128)(2,1)}) %all-gather.3.cloned.1.call-update) | async-done | bytes 5242896 | tf_op jit(solution)/shard_map/all_gather | solution.py:530
  100.5 6.1 %values.1 = (bf16[64,16,128]{2,1,0:T(8,128)(2,1)}, bf16[5120,128]{1,0:T(8,128)(2,1)}) custom-call(s32[3]{0:T(128)} %pad_add_fusion.1.place_ref, s32[4,128]{1,0:T(4,128)} %get-tuple-element.47.slot_ref, bf16[512,5120]{1,0:T(8,128)(2,1)} %all-gather.3.cloned.1.call-done.x_ref, bf16[8,80,128]{2,1,0:T(8,128)(2,1)} %copy-done.16, bf16[8,80,128]{2,1,0:T(8,128)(2,1)} %copy-done.20, ...), custom_call_target="tpu_custom_call" | custom-call | flops 800000000 | bytes 8000000 | tf_op jit(solution)/shard_map/values/pallas_call | solution.py:143
  106.6 7.7 %all-to-all-done = bf16[256,48,128]{2,1,0:T(8,128)(2,1)} async-done(((bf16[256,48,128]{2,1,0:T(8,128)(2,1)}), bf16[256,48,128]{2,1,0:T(8,128)(2,1)}, u32[]{:S(2)}, u32[]{:S(2)}) %all-to-all-start) | async-done | bytes 3145760 | tf_op jit(solution)/shard_map/all_to_all | solution.py:524
  114.2 8.0 %probs.1 = (bf16[64,32,128]{2,1,0:T(8,128)(2,1)}, bf16[4,640,128]{2,1,0:T(8,128)(2,1)}, bf16[512,128]{1,0:T(8,128)(2,1)}, bf16[4,640,128]{2,1,0:T(8,128)(2,1)}, ...) custom-call(s32[3]{0:T(128)} %bitcast.76, ...), custom_call_target="tpu_custom_call" | custom-call | flops 3000000000 | bytes 9000000 | tf_op jit(solution)/shard_map/probs/pallas_call | solution.py:254
  122.2 6.3 %all-to-all-start.1 = ((bf16[64,32,128]{2,1,0:T(8,128)(2,1)}), bf16[64,32,128]{2,1,0:T(8,128)(2,1)S(1)}, u32[]{:S(2)}, u32[]{:S(2)}) async-start(bf16[64,32,128]{2,1,0:T(8,128)(2,1)} %get-tuple-element.38), calls=%async_computation.1 | async-start | bytes 1048576 | tf_op jit(solution)/shard_map/all_to_all | solution.py:541
  128.7 8.0 %turn.1.x_ref = bf16[5120,512]{1,0:T(8,128)(2,1)} custom-call(bf16[512,5120]{1,0:T(8,128)(2,1)} %all-gather.3.cloned.1.call-done.x_ref), custom_call_target="tpu_custom_call" | custom-call | flops 1000000 | bytes 11000000 | tf_op jit(solution)/shard_map/turn/pallas_call | solution.py:164
  136.7 8.7 %all-to-all-done.1.r_ref = bf16[64,32,128]{2,1,0:T(8,128)(2,1)S(1)} async-done(((bf16[64,32,128]{2,1,0:T(8,128)(2,1)}), bf16[64,32,128]{2,1,0:T(8,128)(2,1)S(1)}, u32[]{:S(2)}, u32[]{:S(2)}) %all-to-all-start.1) | async-done | bytes 524320 | tf_op jit(solution)/shard_map/all_to_all | solution.py:541
  145.4 6.0 %grads.1 = bf16[64,4,24,128]{3,2,1,0:T(8,128)(2,1)} custom-call(s32[4,128]{1,0:T(4,128)S(1)} %copy-done.1, bf16[64,32,128]{2,1,0:T(8,128)(2,1)S(1)} %all-to-all-done.1.r_ref, bf16[4,640,128]{2,1,0:T(8,128)(2,1)S(1)} %copy-done.7, bf16[512,128]{1,0:T(8,128)(2,1)S(1)} %copy-done.13, bf16[4,640,128]{2,1,0:T(8,128)(2,1)S(1)} %copy-done.8, ...), custom_call_target="tpu_custom_call" | custom-call | flops 3000000000 | bytes 8000000 | tf_op jit(solution)/shard_map/grads/pallas_call | solution.py:327
  151.5 8.0 %all-to-all-start.2 = ((bf16[256,24,128]{2,1,0:T(8,128)(2,1)}), bf16[256,24,128]{2,1,0:T(8,128)(2,1)S(1)}, u32[]{:S(2)}, u32[]{:S(2)}) async-start(bf16[256,24,128]{2,1,0:T(8,128)(2,1)} %bitcast.25), calls=%async_computation.2 | async-start | bytes 3145728 | tf_op jit(solution)/shard_map/all_to_all | solution.py:548
  159.4 5.7 %weight_terms.1 = (bf16[512,128]{1,0:T(8,128)(2,1)}, bf16[2,4,8,80,128]{4,3,2,1,0:T(8,128)(2,1)}) custom-call(s32[4,128]{1,0:T(4,128)} %get-tuple-element.47.slot_ref, bf16[64,32,128]{2,1,0:T(8,128)(2,1)} %copy-done, bf16[5120,512]{1,0:T(8,128)(2,1)} %turn.1.x_ref), custom_call_target="tpu_custom_call" | custom-call | flops 800000000 | bytes 7000000 | tf_op jit(solution)/shard_map/weight_terms/pallas_call | solution.py:373
  179.9 4.0 %collective-permute-done.15 = bf16[8,80,128]{2,1,0:T(8,128)(2,1)S(1)} collective-permute-done((bf16[8,80,128]{2,1,0:T(8,128)(2,1)S(1)}, bf16[8,80,128]{2,1,0:T(8,128)(2,1)S(1)}, u32[]{:S(2)}, u32[]{:S(2)}) %collective-permute-start.15) | collective-permute-done | bytes 163872 | tf_op jit(solution)/shard_map/ppermute | solution.py:471
  183.9 5.9 %collective-permute-done.16 = bf16[8,80,128]{2,1,0:T(8,128)(2,1)S(1)} collective-permute-done((bf16[8,80,128]{2,1,0:T(8,128)(2,1)S(1)}, bf16[8,80,128]{2,1,0:T(8,128)(2,1)S(1)}, u32[]{:S(2)}, u32[]{:S(2)}) %collective-permute-start.16) | collective-permute-done | bytes 163872 | tf_op jit(solution)/shard_map/ppermute | solution.py:471
  189.9 6.1 %grad_x.1 = bf16[128,5120]{1,0:T(8,128)(2,1)} custom-call(bf16[4,128,128]{2,1,0:T(8,128)(2,1)} %select_select_fusion.1.dv_ref, bf16[4,5120,128]{2,1,0:T(8,128)(2,1)} %bitcast.71), custom_call_target="tpu_custom_call" | custom-call | flops 700000000 | bytes 7000000 | tf_op jit(solution)/shard_map/grad_x/pallas_call | solution.py:404
  196.0 4.9 %all-to-all-done.2 = bf16[256,24,128]{2,1,0:T(8,128)(2,1)S(1)} async-done(((bf16[256,24,128]{2,1,0:T(8,128)(2,1)}), bf16[256,24,128]{2,1,0:T(8,128)(2,1)S(1)}, u32[]{:S(2)}, u32[]{:S(2)}) %all-to-all-start.2) | async-done | bytes 1572896 | tf_op jit(solution)/shard_map/all_to_all | solution.py:548
  201.4 4.1 %collective-permute-done.21 = bf16[4,80,128]{2,1,0:T(8,128)(2,1)S(1)} collective-permute-done((bf16[4,80,128]{2,1,0:T(8,128)(2,1)S(1)}, bf16[4,80,128]{2,1,0:T(8,128)(2,1)S(1)}, u32[]{:S(2)}, u32[]{:S(2)}) %collective-permute-start.21) | collective-permute-done | bytes 81952 | tf_op jit(solution)/shard_map/ppermute | solution.py:513
  207.2 3.3 %collective-permute-start.23 = (bf16[80,128]{1,0:T(8,128)(2,1)S(1)}, bf16[80,128]{1,0:T(8,128)(2,1)S(1)}, u32[]{:S(2)}, u32[]{:S(2)}) collective-permute-start(bf16[80,128]{1,0:T(8,128)(2,1)S(1)} %get-tuple-element.75), channel_id=1, source_target_pairs={{0,128},{4,132},{8,136},{12,140},{16,144},{20,148},{24,152},{28,15... | collective-permute-start | bytes 61448 | tf_op jit(solution)/shard_map/ppermute | solution.py:513
  219.0 3.0 %unpack.1 = (bf16[128,2560]{1,0:T(8,128)(2,1)}, bf16[128,512]{1,0:T(8,128)(2,1)}) custom-call(s32[1,128]{1,0:T(1,128)} %copy-done.2, bf16[64,4,24,128]{3,2,1,0:T(8,128)(2,1)} %bitcast.72), custom_call_target="tpu_custom_call" | custom-call | flops 500000000 | bytes 4000000 | tf_op jit(solution)/shard_map/unpack/pallas_call | solution.py:445
  (137 shorter events, 45.2 us)
Async XLA Ops:
  7.2 93.2 %all-gather.3.cloned.1.call-start = ((), (), s32[]{:S(2)}) async-start(), calls=%async_computation.3 | async-start | bytes 6553600 | tf_op jit(solution)/shard_map/all_gather | solution.py:530
  8.7 11.3 %collective-permute-start = (bf16[80,128]{1,0:T(8,128)(2,1)S(1)}, bf16[80,128]{1,0:T(8,128)(2,1)S(1)}, u32[]{:S(2)}, u32[]{:S(2)}) collective-permute-start(bf16[80,128]{1,0:T(8,128)(2,1)S(1)} %constant_dynamic-slice_fusion), channel_id=1, source_target_pairs={{0,128},{4,132},{8,136},{12,140},{16,144},{20,148},{24,152},{28,15... | collective-permute-start | bytes 61448 | tf_op jit(solution)/shard_map/ppermute | solution.py:513
  27.0 87.2 %all-to-all-start = ((bf16[256,48,128]{2,1,0:T(8,128)(2,1)}), bf16[256,48,128]{2,1,0:T(8,128)(2,1)}, u32[]{:S(2)}, u32[]{:S(2)}) async-start(bf16[256,48,128]{2,1,0:T(8,128)(2,1)} %bitcast.5), calls=%async_computation | async-start | bytes 6291456 | tf_op jit(solution)/shard_map/all_to_all | solution.py:524
  40.2 149.6 %all-gather.5.cloned.1.call-start = ((), (), s32[]{:S(2)}) async-start(), calls=%async_computation.4 | async-start | bytes 6553600 | tf_op jit(solution)/shard_map/all_gather | solution.py:537
  40.4 9.3 %collective-permute-start.4 = (s32[2,128]{1,0:T(2,128)S(1)}, s32[2,128]{1,0:T(2,128)S(1)}, u32[]{:S(2)}, u32[]{:S(2)}) collective-permute-start(s32[2,128]{1,0:T(2,128)S(1)} %pad_add_fusion), channel_id=1, source_target_pairs={{0,3},{1,0},{2,1},{3,2},{4,7},{5,4},{6,5},{7,6},{8,11},{9,8},{10,9... | collective-permute-start | bytes 3080 | tf_op jit(solution)/shard_map/ppermute | solution.py:479
  43.3 8.5 %collective-permute-start.5 = (s32[2,128]{1,0:T(2,128)S(1)}, s32[2,128]{1,0:T(2,128)S(1)}, u32[]{:S(2)}, u32[]{:S(2)}) collective-permute-start(s32[2,128]{1,0:T(2,128)S(1)} %pad_add_fusion), channel_id=1, source_target_pairs={{0,2},{1,3},{2,0},{3,1},{4,6},{5,7},{6,4},{7,5},{8,10},{9,11},{10,... | collective-permute-start | bytes 3080 | tf_op jit(solution)/shard_map/ppermute | solution.py:479
  44.1 7.8 %collective-permute-start.6 = (s32[2,128]{1,0:T(2,128)S(1)}, s32[2,128]{1,0:T(2,128)S(1)}, u32[]{:S(2)}, u32[]{:S(2)}) collective-permute-start(s32[2,128]{1,0:T(2,128)S(1)} %pad_add_fusion), channel_id=1, source_target_pairs={{0,1},{1,2},{2,3},{3,0},{4,5},{5,6},{6,7},{7,4},{8,9},{9,10},{10,1... | collective-permute-start | bytes 3080 | tf_op jit(solution)/shard_map/ppermute | solution.py:479
  45.6 10.7 %collective-permute-start.10 = (bf16[8,80,128]{2,1,0:T(8,128)(2,1)S(1)}, bf16[8,80,128]{2,1,0:T(8,128)(2,1)S(1)}, u32[]{:S(2)}, u32[]{:S(2)}) collective-permute-start(bf16[8,80,128]{2,1,0:T(8,128)(2,1)S(1)} %constant_dynamic-update-slice_fusion.refs_0_), channel_id=1, source_target_pairs={{0,16},{4,20},{8,24},{12,28},{16,0},{20,4},{24,8},{28,12},{32,48},... | collective-permute-start | bytes 491528 | tf_op jit(solution)/shard_map/ppermute | solution.py:471
  48.6 14.7 %collective-permute-start.12 = (bf16[8,80,128]{2,1,0:T(8,128)(2,1)S(1)}, bf16[8,80,128]{2,1,0:T(8,128)(2,1)S(1)}, u32[]{:S(2)}, u32[]{:S(2)}) collective-permute-start(bf16[8,80,128]{2,1,0:T(8,128)(2,1)S(1)} %constant_dynamic-update-slice_fusion.refs_0_), channel_id=1, source_target_pairs={{0,24},{4,28},{8,0},{12,4},{16,8},{20,12},{24,16},{28,20},{32,56},... | collective-permute-start | bytes 491528 | tf_op jit(solution)/shard_map/ppermute | solution.py:471
  49.7 13.6 %collective-permute-start.8 = (bf16[8,80,128]{2,1,0:T(8,128)(2,1)S(1)}, bf16[8,80,128]{2,1,0:T(8,128)(2,1)S(1)}, u32[]{:S(2)}, u32[]{:S(2)}) collective-permute-start(bf16[8,80,128]{2,1,0:T(8,128)(2,1)S(1)} %constant_dynamic-update-slice_fusion.refs_0_), channel_id=1, source_target_pairs={{0,8},{4,12},{8,16},{12,20},{16,24},{20,28},{24,0},{28,4},{32,40},... | collective-permute-start | bytes 491528 | tf_op jit(solution)/shard_map/ppermute | solution.py:471
  51.8 12.6 %collective-permute-start.7 = (bf16[8,80,128]{2,1,0:T(8,128)(2,1)S(1)}, bf16[8,80,128]{2,1,0:T(8,128)(2,1)S(1)}, u32[]{:S(2)}, u32[]{:S(2)}) collective-permute-start(bf16[8,80,128]{2,1,0:T(8,128)(2,1)S(1)} %constant_dynamic-update-slice_fusion.refs_0_), channel_id=1, source_target_pairs={{0,4},{4,0},{8,12},{12,8},{16,20},{20,16},{24,28},{28,24},{32,36},... | collective-permute-start | bytes 491528 | tf_op jit(solution)/shard_map/ppermute | solution.py:475
  56.2 8.2 %collective-permute-start.11 = (bf16[8,80,128]{2,1,0:T(8,128)(2,1)S(1)}, bf16[8,80,128]{2,1,0:T(8,128)(2,1)S(1)}, u32[]{:S(2)}, u32[]{:S(2)}) collective-permute-start(bf16[8,80,128]{2,1,0:T(8,128)(2,1)S(1)} %collective-permute-done.10.refs_4_), channel_id=1, source_target_pairs={{0,4},{4,0},{8,12},{12,8},{16,20},{20,16},{24,28},{28,24},{32,36},... | collective-permute-start | bytes 491528 | tf_op jit(solution)/shard_map/ppermute | solution.py:475
  122.2 23.1 %all-to-all-start.1 = ((bf16[64,32,128]{2,1,0:T(8,128)(2,1)}), bf16[64,32,128]{2,1,0:T(8,128)(2,1)S(1)}, u32[]{:S(2)}, u32[]{:S(2)}) async-start(bf16[64,32,128]{2,1,0:T(8,128)(2,1)} %get-tuple-element.38), calls=%async_computation.1 | async-start | bytes 1048576 | tf_op jit(solution)/shard_map/all_to_all | solution.py:541
  151.5 49.4 %all-to-all-start.2 = ((bf16[256,24,128]{2,1,0:T(8,128)(2,1)}), bf16[256,24,128]{2,1,0:T(8,128)(2,1)S(1)}, u32[]{:S(2)}, u32[]{:S(2)}) async-start(bf16[256,24,128]{2,1,0:T(8,128)(2,1)} %bitcast.25), calls=%async_computation.2 | async-start | bytes 3145728 | tf_op jit(solution)/shard_map/all_to_all | solution.py:548
  168.2 9.1 %collective-permute-start.18 = (bf16[128,128]{1,0:T(8,128)(2,1)S(1)}, bf16[128,128]{1,0:T(8,128)(2,1)S(1)}, u32[]{:S(2)}, u32[]{:S(2)}) collective-permute-start(bf16[128,128]{1,0:T(8,128)(2,1)S(1)} %get-tuple-element.69), channel_id=1, source_target_pairs={{0,3},{1,0},{2,1},{3,2},{4,7},{5,4},{6,5},{7,6},{8,11},{9,8},{10,9... | collective-permute-start | bytes 98312 | tf_op jit(solution)/shard_map/ppermute | solution.py:479
  171.2 7.6 %collective-permute-start.19 = (bf16[128,128]{1,0:T(8,128)(2,1)S(1)}, bf16[128,128]{1,0:T(8,128)(2,1)S(1)}, u32[]{:S(2)}, u32[]{:S(2)}) collective-permute-start(bf16[128,128]{1,0:T(8,128)(2,1)S(1)} %get-tuple-element.72), channel_id=1, source_target_pairs={{0,2},{1,3},{2,0},{3,1},{4,6},{5,7},{6,4},{7,5},{8,10},{9,11},{10,... | collective-permute-start | bytes 98312 | tf_op jit(solution)/shard_map/ppermute | solution.py:479
  171.9 7.2 %collective-permute-start.20 = (bf16[128,128]{1,0:T(8,128)(2,1)S(1)}, bf16[128,128]{1,0:T(8,128)(2,1)S(1)}, u32[]{:S(2)}, u32[]{:S(2)}) collective-permute-start(bf16[128,128]{1,0:T(8,128)(2,1)S(1)} %get-tuple-element.71), channel_id=1, source_target_pairs={{0,1},{1,2},{2,3},{3,0},{4,5},{5,6},{6,7},{7,4},{8,9},{9,10},{10,1... | collective-permute-start | bytes 98312 | tf_op jit(solution)/shard_map/ppermute | solution.py:479
  173.1 10.8 %collective-permute-start.15 = (bf16[8,80,128]{2,1,0:T(8,128)(2,1)S(1)}, bf16[8,80,128]{2,1,0:T(8,128)(2,1)S(1)}, u32[]{:S(2)}, u32[]{:S(2)}) collective-permute-start(bf16[8,80,128]{2,1,0:T(8,128)(2,1)S(1)} %get-tuple-element.62), channel_id=1, source_target_pairs={{0,8},{4,12},{8,16},{12,20},{16,24},{20,28},{24,0},{28,4},{32,40},... | collective-permute-start | bytes 491528 | tf_op jit(solution)/shard_map/ppermute | solution.py:471
  174.7 15.1 %collective-permute-start.16 = (bf16[8,80,128]{2,1,0:T(8,128)(2,1)S(1)}, bf16[8,80,128]{2,1,0:T(8,128)(2,1)S(1)}, u32[]{:S(2)}, u32[]{:S(2)}) collective-permute-start(bf16[8,80,128]{2,1,0:T(8,128)(2,1)S(1)} %get-tuple-element.64), channel_id=1, source_target_pairs={{0,16},{4,20},{8,24},{12,28},{16,0},{20,4},{24,8},{28,12},{32,48},... | collective-permute-start | bytes 491528 | tf_op jit(solution)/shard_map/ppermute | solution.py:471
  177.3 12.4 %collective-permute-start.17 = (bf16[8,80,128]{2,1,0:T(8,128)(2,1)S(1)}, bf16[8,80,128]{2,1,0:T(8,128)(2,1)S(1)}, u32[]{:S(2)}, u32[]{:S(2)}) collective-permute-start(bf16[8,80,128]{2,1,0:T(8,128)(2,1)S(1)} %get-tuple-element.63), channel_id=1, source_target_pairs={{0,24},{4,28},{8,0},{12,4},{16,8},{20,12},{24,16},{28,20},{32,56},... | collective-permute-start | bytes 491528 | tf_op jit(solution)/shard_map/ppermute | solution.py:471
  205.5 6.6 %collective-permute-start.22 = (bf16[80,128]{1,0:T(8,128)(2,1)S(1)}, bf16[80,128]{1,0:T(8,128)(2,1)S(1)}, u32[]{:S(2)}, u32[]{:S(2)}) collective-permute-start(bf16[80,128]{1,0:T(8,128)(2,1)S(1)} %get-tuple-element.73), channel_id=1, source_target_pairs={{0,64},{4,68},{8,72},{12,76},{16,80},{20,84},{24,88},{28,92},{32,9... | collective-permute-start | bytes 61448 | tf_op jit(solution)/shard_map/ppermute | solution.py:513
  207.2 7.7 %collective-permute-start.23 = (bf16[80,128]{1,0:T(8,128)(2,1)S(1)}, bf16[80,128]{1,0:T(8,128)(2,1)S(1)}, u32[]{:S(2)}, u32[]{:S(2)}) collective-permute-start(bf16[80,128]{1,0:T(8,128)(2,1)S(1)} %get-tuple-element.75), channel_id=1, source_target_pairs={{0,128},{4,132},{8,136},{12,140},{16,144},{20,148},{24,152},{28,15... | collective-permute-start | bytes 61448 | tf_op jit(solution)/shard_map/ppermute | solution.py:513
  210.4 5.9 %collective-permute-start.24 = (bf16[80,128]{1,0:T(8,128)(2,1)S(1)}, bf16[80,128]{1,0:T(8,128)(2,1)S(1)}, u32[]{:S(2)}, u32[]{:S(2)}) collective-permute-start(bf16[80,128]{1,0:T(8,128)(2,1)S(1)} %get-tuple-element.74), channel_id=1, source_target_pairs={{0,192},{4,196},{8,200},{12,204},{16,208},{20,212},{24,216},{28,22... | collective-permute-start | bytes 61448 | tf_op jit(solution)/shard_map/ppermute | solution.py:513
  216.3 5.7 %collective-permute-start.25 = (f32[80,128]{1,0:T(8,128)S(1)}, f32[80,128]{1,0:T(8,128)S(1)}, u32[]{:S(2)}, u32[]{:S(2)}) collective-permute-start(f32[80,128]{1,0:T(8,128)S(1)} %fusion.7), channel_id=1, source_target_pairs={{0,3},{1,0},{2,1},{3,2},{4,7},{5,4},{6,5},{7,6},{8,11},{9,8},{10,9... | collective-permute-start | bytes 122888 | tf_op jit(solution)/shard_map/ppermute | solution.py:479
  (36 other events, 541.1 us)
Sparse Core Ops, SparseCore 0:
  9.9 90.5 all-gather.2
  106.7 72.7 all-gather.4

commit v2 on v1

--- a/solution.py
+++ b/solution.py
@@ -75,22 +75,23 @@
     def chunk(s, m):
         if m < PER:
             return q_ref[:, s * QW + m * HEAD : s * QW + (m + 1) * HEAD]
-        if m < 2 * PER + 1 and m > PER:
-            at = s * QW + (m - PER - 1) * HEAD
-            return (coef * g_ref[:, at : at + HEAD].astype(F32)).astype(BF)
-        return k_ref[:, s * HEAD : (s + 1) * HEAD]
-
-    for t in range(3):
+        if m == PER:
+            return k_ref[:, s * HEAD : (s + 1) * HEAD]
+        at = s * QW + (m - PER - 1) * HEAD
+        return (coef * g_ref[:, at : at + HEAD].astype(F32)).astype(BF)
+
+    flat = out_ref.reshape(16, NS, 44, HEAD)
+    for begin in (0, 4, 7):
         rhs = jnp.concatenate(
             [
-                jnp.concatenate([chunk(s, 4 * t + m) for m in range(4)], axis=0)
+                jnp.concatenate([chunk(s, begin + m) for m in range(4)], axis=0)
                 for s in range(NS)
             ],
             axis=1,
         )
         res = mm(onehot, rhs).astype(BF)
         for s in range(NS):
-            out_ref[:, s, 16 * t : 16 * t + 16, :] = res[:, s * HEAD : (s + 1) * HEAD].reshape(
+            flat[:, s, 4 * begin : 4 * begin + 16, :] = res[:, s * HEAD : (s + 1) * HEAD].reshape(
                 16, 16, HEAD
             )
 
@@ -99,7 +100,7 @@
     return pl.pallas_call(
         pack_rows_kernel,
         grid=(4,),
-        out_shape=jax.ShapeDtypeStruct((NDP, NS, 48, HEAD), BF),
+        out_shape=jax.ShapeDtypeStruct((NDP, NS, 11, CAP, HEAD), BF),
         in_specs=[
             pl.BlockSpec((1, ROWS), lambda i: (0, 0)),
             pl.BlockSpec((1, ROWS), lambda i: (0, 0)),
@@ -107,7 +108,7 @@
             pl.BlockSpec((ROWS, NS * HEAD), lambda i: (0, 0)),
             pl.BlockSpec((ROWS, NS * QW), lambda i: (0, 0)),
         ],
-        out_specs=pl.BlockSpec((16, NS, 48, HEAD), lambda i: (i, 0, 0, 0)),
+        out_specs=pl.BlockSpec((16, NS, 11, CAP, HEAD), lambda i: (i, 0, 0, 0, 0)),
         compiler_params=params(SMALL),
         cost_estimate=cost(1.6e9, 5e6),
         name="pack_rows",
@@ -191,13 +192,14 @@
     lane = lax.broadcasted_iota(jnp.int32, (1, NDP * 16), 1)
     wanted = (lane // 16) * CAP + lane % 4
     place = (lane % 16) // 4
+    flat = r_ref.reshape(NDP, NS, 44, HEAD)
     for s in range(NS):
         own = slot_column(slot_ref[s : s + 1, :])
         pick = jnp.concatenate(
             [ones_where(jnp.where(place == m, wanted, -1) == own) for m in range(4)], axis=0
         )
         rhs = jnp.concatenate(
-            [r_ref[:, s, 16 * t : 16 * t + 16, :].reshape(NDP * 16, HEAD) for t in range(3)],
+            [flat[:, s, 4 * b : 4 * b + 16, :].reshape(NDP * 16, HEAD) for b in (0, 4, 7)],
             axis=1,
         )
         res = mm(pick, rhs).astype(BF)
@@ -205,7 +207,7 @@
         qs[s, 512:640, :] = res[0:128, 128:256]
         ks[s * ROWS : (s + 1) * ROWS, :] = res[128:256, 128:256]
         ds[s, 0:256, :] = res[256:512, 128:256]
-        ds[s, 256:640, :] = res[0:384, 256:384]
+        ds[s, 256:640, :] = res[128:512, 256:384]
         send(qs.at[s], qs_out.at[s])
         send(ds.at[s], ds_out.at[s])
     send(ks, ks_out)
@@ -522,7 +524,7 @@
     rows = pack_rows(own_slot, token_coef[None], q_saved, k_saved, grad_attn)
     rows, slots, stage = lax.optimization_barrier((rows, slots, stage))
     arrived = lax.all_to_all(
-        rows.reshape(NDP * NS, 48, HEAD), ("dp", "seq"), split_axis=0, concat_axis=0, tiled=True
+        rows.reshape(NDP * NS, 11, CAP, HEAD), ("dp", "seq"), split_axis=0, concat_axis=0, tiled=True
     )
 
     all_slots = in_order([slots] + [along_seq(slots, d) for d in range(1, NS)], seq)
@@ -537,7 +539,7 @@
     w_all = lax.all_gather(head_w, "seq", axis=0, tiled=True)
 
     arrived, recv_all, v_out = lax.optimization_barrier((arrived, recv_all, v_out))
-    both, *kept = probs_of(lengths[0], recv_all, arrived.reshape(NDP, NS, 48, HEAD), v_out)
+    both, *kept = probs_of(lengths[0], recv_all, arrived.reshape(NDP, NS, 11, CAP, HEAD), v_out)
     both = lax.all_to_all(both, "dp", split_axis=0, concat_axis=0, tiled=True)
     x_turned = turn(x_all)
     both, x_turned = lax.optimization_barrier((both, x_turned))
@@ -569,10 +571,11 @@
     for bits in (1, 2, 3):
         total = total + across_z(pick(half, (z // 2) ^ bits), 2 * bits).astype(F32)
     own = total / math.sqrt(GROUP * NDP)
+    grad_q, grad_k = unpack(own_slot, dqk_back.reshape(NDP, NS, 24, HEAD))
+    own, grad_q, grad_k = lax.optimization_barrier((own, grad_q, grad_k))
     heads = in_order([own] + [along_seq(own, d) for d in range(1, NS)], seq)
     grad_v_weight = jnp.concatenate([heads[s] for s in range(NS)], axis=1)
 
-    grad_q, grad_k = unpack(own_slot, dqk_back.reshape(NDP, NS, 24, HEAD))
     return (grad_x, grad_q, grad_k, grad_v_weight)
 
 

time: 232 us -> 231 us (level)
  waiting for transfers between devices: 94.1 us -> 88.7 us
  starting transfers between devices: 67.9 us -> 72.2 us
    all_to_all x1, waiting for transfers between devices: 7.69 us -> 2.31 us  [shards(): lax.all_to_all(rows.reshape(NDP * NS, 11, CAP, HEAD), ('dp', 'seq'), spli...]
    all_to_all x1, starting transfers between devices: 6.34 us -> 10 us  [shards(): both = lax.all_to_all(both, 'dp', split_axis=0, concat_axis=0, tiled=True)]
    ppermute x8, waiting for transfers between devices: 11.6 us -> 8.5 us  [across_z(): return lax.ppermute(value, 'dp', swap)]
where the time goes in v2:
time: 231 us; the launch traced here: 230 us
  waiting for transfers between devices  88.7 us (38%)
  starting transfers between devices  72.2 us (31%)
  Pallas kernels  46.6 us (20%)
  between operations  14.6 us (6%)
  local copies, waits for them, and re-layouts  5.31 us (2%)
  other arithmetic  2.95 us (1%)
    all_gather x1, waiting for transfers between devices, shards(): x_all = lax.all_gather(x_saved, 'seq', axis=0, tiled=True)  36 us
    ppermute x6, waiting for transfers between devices, along_x(): lax.ppermute(value, 'dp', [(dp_of(z, x, c), dp_of(z, (x + d) % NX, c)) fo...  21.8 us
    ppermute x8, starting transfers between devices, across_z(): return lax.ppermute(value, 'dp', swap)  17.1 us
    all_to_all x1, starting transfers between devices, shards(): lax.all_to_all(rows.reshape(NDP * NS, 11, CAP, HEAD), ('dp', 'seq'), spli...  13 us
    ppermute x9, starting transfers between devices, along_seq(): return lax.ppermute(value, 'seq', [(s, (s + d) % NS) for s in range(NS)])  11.9 us
    ppermute x6, starting transfers between devices, along_x(): lax.ppermute(value, 'dp', [(dp_of(z, x, c), dp_of(z, (x + d) % NX, c)) fo...  10.7 us
    all_to_all x1, starting transfers between devices, shards(): both = lax.all_to_all(both, 'dp', split_axis=0, concat_axis=0, tiled=True)  10 us
    all_to_all x1, starting transfers between devices, shards(): lax.all_to_all(dqk_out.reshape(NDP * NS, 24, HEAD), ('dp', 'seq'), split_...  8.86 us
  transfers between devices with their start and end apart: 33, of which 20 were waited for; matrix products, arithmetic and copies ran while one was open for 3% of the time, Pallas kernels for 20%

profile of v2, /device:TPU:32, one launch (start us, length us, event | category | flops | bytes accessed | tf_op | source)
XLA Modules:
  0.0 230.4 jit_solution(11067068477010210982)
XLA Ops:
  8.7 6.3 %collective-permute-start = (bf16[80,128]{1,0:T(8,128)(2,1)S(1)}, bf16[80,128]{1,0:T(8,128)(2,1)S(1)}, u32[]{:S(2)}, u32[]{:S(2)}) collective-permute-start(bf16[80,128]{1,0:T(8,128)(2,1)S(1)} %constant_dynamic-slice_fusion), channel_id=1, source_target_pairs={{0,128},{4,132},{8,136},{12,140},{16,144},{20,148},{24,152},{28,15... | collective-permute-start | bytes 61448 | tf_op jit(solution)/shard_map/ppermute | solution.py:515
  16.3 3.8 %pack_rows.1 = bf16[64,4,11,4,128]{4,3,2,1,0:T(4,128)(2,1)} custom-call(s32[1,128]{1,0:T(1,128)S(1)} %add_bitcast_fusion.1.slots_ref.slot_ref, f32[1,128]{1,0:T(1,128)S(1)} %bitcast.70, bf16[128,2560]{1,0:T(8,128)(2,1)S(1)} %copy-done.3, bf16[128,512]{1,0:T(8,128)(2,1)S(1)} %copy-done.5, bf16[128,2560]{1,0:T(8,128)(2,1)S(1)} %copy-done.4), custom_call_target="tpu_custom_call" | custom-call | flops 1600000000 | bytes 5000000 | tf_op jit(solution)/shard_map/pack_rows/pallas_call | solution.py:100
  27.2 13.0 %all-to-all-start = ((bf16[256,11,4,128]{3,2,1,0:T(4,128)(2,1)}), bf16[256,11,4,128]{3,2,1,0:T(4,128)(2,1)}, u32[]{:S(2)}, u32[]{:S(2)}) async-start(bf16[256,11,4,128]{3,2,1,0:T(4,128)(2,1)} %bitcast.5), calls=%async_computation | async-start | bytes 5767168 | tf_op jit(solution)/shard_map/all_to_all | solution.py:526
  40.4 3.0 %collective-permute-start.4 = (s32[2,128]{1,0:T(2,128)S(1)}, s32[2,128]{1,0:T(2,128)S(1)}, u32[]{:S(2)}, u32[]{:S(2)}) collective-permute-start(s32[2,128]{1,0:T(2,128)S(1)} %pad_add_fusion), channel_id=1, source_target_pairs={{0,3},{1,0},{2,1},{3,2},{4,7},{5,4},{6,5},{7,6},{8,11},{9,8},{10,9... | collective-permute-start | bytes 3080 | tf_op jit(solution)/shard_map/ppermute | solution.py:481
  45.6 3.0 %collective-permute-start.10 = (bf16[8,80,128]{2,1,0:T(8,128)(2,1)S(1)}, bf16[8,80,128]{2,1,0:T(8,128)(2,1)S(1)}, u32[]{:S(2)}, u32[]{:S(2)}) collective-permute-start(bf16[8,80,128]{2,1,0:T(8,128)(2,1)S(1)} %constant_dynamic-update-slice_fusion.refs_0_), channel_id=1, source_target_pairs={{0,16},{4,20},{8,24},{12,28},{16,0},{20,4},{24,8},{28,12},{32,48},... | collective-permute-start | bytes 491528 | tf_op jit(solution)/shard_map/ppermute | solution.py:473
  50.7 7.1 %collective-permute-done.10.refs_4_ = bf16[8,80,128]{2,1,0:T(8,128)(2,1)S(1)} collective-permute-done((bf16[8,80,128]{2,1,0:T(8,128)(2,1)S(1)}, bf16[8,80,128]{2,1,0:T(8,128)(2,1)S(1)}, u32[]{:S(2)}, u32[]{:S(2)}) %collective-permute-start.10) | collective-permute-done | bytes 163872 | tf_op jit(solution)/shard_map/ppermute | solution.py:473
  57.8 4.8 %collective-permute-done.12.refs_6_ = bf16[8,80,128]{2,1,0:T(8,128)(2,1)S(1)} collective-permute-done((bf16[8,80,128]{2,1,0:T(8,128)(2,1)S(1)}, bf16[8,80,128]{2,1,0:T(8,128)(2,1)S(1)}, u32[]{:S(2)}, u32[]{:S(2)}) %collective-permute-start.12) | collective-permute-done | bytes 163872 | tf_op jit(solution)/shard_map/ppermute | solution.py:473
  64.2 36.0 %all-gather.3.cloned.1.call-done.x_ref = bf16[512,5120]{1,0:T(8,128)(2,1)} async-done(((bf16[128,5120]{1,0:T(8,128)(2,1)}), bf16[512,5120]{1,0:T(8,128)(2,1)}) %all-gather.3.cloned.1.call-update) | async-done | bytes 5242896 | tf_op jit(solution)/shard_map/all_gather | solution.py:532
  100.3 6.1 %values.1 = (bf16[64,16,128]{2,1,0:T(8,128)(2,1)}, bf16[5120,128]{1,0:T(8,128)(2,1)}) custom-call(s32[3]{0:T(128)} %pad_add_fusion.1.place_ref, s32[4,128]{1,0:T(4,128)} %get-tuple-element.50.slot_ref, bf16[512,5120]{1,0:T(8,128)(2,1)} %all-gather.3.cloned.1.call-done.x_ref, bf16[8,80,128]{2,1,0:T(8,128)(2,1)} %copy-done.16, bf16[8,80,128]{2,1,0:T(8,128)(2,1)} %copy-done.20, ...), custom_call_target="tpu_custom_call" | custom-call | flops 800000000 | bytes 8000000 | tf_op jit(solution)/shard_map/values/pallas_call | solution.py:144
  108.7 7.9 %probs.1 = (bf16[64,32,128]{2,1,0:T(8,128)(2,1)}, bf16[4,640,128]{2,1,0:T(8,128)(2,1)}, bf16[512,128]{1,0:T(8,128)(2,1)}, bf16[4,640,128]{2,1,0:T(8,128)(2,1)}, ...) custom-call(s32[3]{0:T(128)} %bitcast.76, ...), custom_call_target="tpu_custom_call" | custom-call | flops 3000000000 | bytes 9000000 | tf_op jit(solution)/shard_map/probs/pallas_call | solution.py:256
  116.6 10.0 %all-to-all-start.1 = ((bf16[64,32,128]{2,1,0:T(8,128)(2,1)}), bf16[64,32,128]{2,1,0:T(8,128)(2,1)S(1)}, u32[]{:S(2)}, u32[]{:S(2)}) async-start(bf16[64,32,128]{2,1,0:T(8,128)(2,1)} %get-tuple-element.41), calls=%async_computation.1 | async-start | bytes 1048576 | tf_op jit(solution)/shard_map/all_to_all | solution.py:543
  126.8 8.0 %turn.1.x_ref = bf16[5120,512]{1,0:T(8,128)(2,1)} custom-call(bf16[512,5120]{1,0:T(8,128)(2,1)} %all-gather.3.cloned.1.call-done.x_ref), custom_call_target="tpu_custom_call" | custom-call | flops 1000000 | bytes 11000000 | tf_op jit(solution)/shard_map/turn/pallas_call | solution.py:165
  134.7 8.7 %all-to-all-done.1.r_ref = bf16[64,32,128]{2,1,0:T(8,128)(2,1)S(1)} async-done(((bf16[64,32,128]{2,1,0:T(8,128)(2,1)}), bf16[64,32,128]{2,1,0:T(8,128)(2,1)S(1)}, u32[]{:S(2)}, u32[]{:S(2)}) %all-to-all-start.1) | async-done | bytes 524320 | tf_op jit(solution)/shard_map/all_to_all | solution.py:543
  143.5 6.0 %grads.1 = bf16[64,4,24,128]{3,2,1,0:T(8,128)(2,1)} custom-call(s32[4,128]{1,0:T(4,128)S(1)} %copy-done.1, bf16[64,32,128]{2,1,0:T(8,128)(2,1)S(1)} %all-to-all-done.1.r_ref, bf16[4,640,128]{2,1,0:T(8,128)(2,1)S(1)} %copy-done.7, bf16[512,128]{1,0:T(8,128)(2,1)S(1)} %copy-done.13, bf16[4,640,128]{2,1,0:T(8,128)(2,1)S(1)} %copy-done.8, ...), custom_call_target="tpu_custom_call" | custom-call | flops 3000000000 | bytes 8000000 | tf_op jit(solution)/shard_map/grads/pallas_call | solution.py:329
  149.5 8.9 %all-to-all-start.2 = ((bf16[256,24,128]{2,1,0:T(8,128)(2,1)}), bf16[256,24,128]{2,1,0:T(8,128)(2,1)S(1)}, u32[]{:S(2)}, u32[]{:S(2)}) async-start(bf16[256,24,128]{2,1,0:T(8,128)(2,1)} %bitcast.25), calls=%async_computation.2 | async-start | bytes 3145728 | tf_op jit(solution)/shard_map/all_to_all | solution.py:550
  158.4 5.7 %weight_terms.1 = (bf16[512,128]{1,0:T(8,128)(2,1)}, bf16[2,4,8,80,128]{4,3,2,1,0:T(8,128)(2,1)}) custom-call(s32[4,128]{1,0:T(4,128)} %get-tuple-element.50.slot_ref, bf16[64,32,128]{2,1,0:T(8,128)(2,1)} %copy-done, bf16[5120,512]{1,0:T(8,128)(2,1)} %turn.1.x_ref), custom_call_target="tpu_custom_call" | custom-call | flops 800000000 | bytes 7000000 | tf_op jit(solution)/shard_map/weight_terms/pallas_call | solution.py:375
  167.2 3.0 %collective-permute-start.18 = (bf16[128,128]{1,0:T(8,128)(2,1)S(1)}, bf16[128,128]{1,0:T(8,128)(2,1)S(1)}, u32[]{:S(2)}, u32[]{:S(2)}) collective-permute-start(bf16[128,128]{1,0:T(8,128)(2,1)S(1)} %get-tuple-element.75), channel_id=1, source_target_pairs={{0,3},{1,0},{2,1},{3,2},{4,7},{5,4},{6,5},{7,6},{8,11},{9,8},{10,9... | collective-permute-start | bytes 98312 | tf_op jit(solution)/shard_map/ppermute | solution.py:481
  179.0 3.8 %collective-permute-done.15 = bf16[8,80,128]{2,1,0:T(8,128)(2,1)S(1)} collective-permute-done((bf16[8,80,128]{2,1,0:T(8,128)(2,1)S(1)}, bf16[8,80,128]{2,1,0:T(8,128)(2,1)S(1)}, u32[]{:S(2)}, u32[]{:S(2)}) %collective-permute-start.15) | collective-permute-done | bytes 163872 | tf_op jit(solution)/shard_map/ppermute | solution.py:473
  182.8 5.9 %collective-permute-done.16 = bf16[8,80,128]{2,1,0:T(8,128)(2,1)S(1)} collective-permute-done((bf16[8,80,128]{2,1,0:T(8,128)(2,1)S(1)}, bf16[8,80,128]{2,1,0:T(8,128)(2,1)S(1)}, u32[]{:S(2)}, u32[]{:S(2)}) %collective-permute-start.16) | collective-permute-done | bytes 163872 | tf_op jit(solution)/shard_map/ppermute | solution.py:473
  188.8 6.1 %grad_x.1 = bf16[128,5120]{1,0:T(8,128)(2,1)} custom-call(bf16[4,128,128]{2,1,0:T(8,128)(2,1)} %select_select_fusion.1.dv_ref, bf16[4,5120,128]{2,1,0:T(8,128)(2,1)} %bitcast.71), custom_call_target="tpu_custom_call" | custom-call | flops 700000000 | bytes 7000000 | tf_op jit(solution)/shard_map/grad_x/pallas_call | solution.py:406
  194.9 4.9 %all-to-all-done.2 = bf16[256,24,128]{2,1,0:T(8,128)(2,1)S(1)} async-done(((bf16[256,24,128]{2,1,0:T(8,128)(2,1)}), bf16[256,24,128]{2,1,0:T(8,128)(2,1)S(1)}, u32[]{:S(2)}, u32[]{:S(2)}) %all-to-all-start.2) | async-done | bytes 1572896 | tf_op jit(solution)/shard_map/all_to_all | solution.py:550
  200.4 4.1 %collective-permute-done.21 = bf16[4,80,128]{2,1,0:T(8,128)(2,1)S(1)} collective-permute-done((bf16[4,80,128]{2,1,0:T(8,128)(2,1)S(1)}, bf16[4,80,128]{2,1,0:T(8,128)(2,1)S(1)}, u32[]{:S(2)}, u32[]{:S(2)}) %collective-permute-start.21) | collective-permute-done | bytes 81952 | tf_op jit(solution)/shard_map/ppermute | solution.py:515
  206.1 3.3 %collective-permute-start.23 = (bf16[80,128]{1,0:T(8,128)(2,1)S(1)}, bf16[80,128]{1,0:T(8,128)(2,1)S(1)}, u32[]{:S(2)}, u32[]{:S(2)}) collective-permute-start(bf16[80,128]{1,0:T(8,128)(2,1)S(1)} %get-tuple-element.81), channel_id=1, source_target_pairs={{0,128},{4,132},{8,136},{12,140},{16,144},{20,148},{24,152},{28,15... | collective-permute-start | bytes 61448 | tf_op jit(solution)/shard_map/ppermute | solution.py:515
  211.1 3.1 %unpack.1 = (bf16[128,2560]{1,0:T(8,128)(2,1)}, bf16[128,512]{1,0:T(8,128)(2,1)}) custom-call(s32[1,128]{1,0:T(1,128)} %copy-done.2, bf16[64,4,24,128]{3,2,1,0:T(8,128)(2,1)} %bitcast.72), custom_call_target="tpu_custom_call" | custom-call | flops 500000000 | bytes 4000000 | tf_op jit(solution)/shard_map/unpack/pallas_call | solution.py:447
  (137 shorter events, 43.5 us)
Async XLA Ops:
  7.2 93.1 %all-gather.3.cloned.1.call-start = ((), (), s32[]{:S(2)}) async-start(), calls=%async_computation.3 | async-start | bytes 6553600 | tf_op jit(solution)/shard_map/all_gather | solution.py:532
  8.7 11.4 %collective-permute-start = (bf16[80,128]{1,0:T(8,128)(2,1)S(1)}, bf16[80,128]{1,0:T(8,128)(2,1)S(1)}, u32[]{:S(2)}, u32[]{:S(2)}) collective-permute-start(bf16[80,128]{1,0:T(8,128)(2,1)S(1)} %constant_dynamic-slice_fusion), channel_id=1, source_target_pairs={{0,128},{4,132},{8,136},{12,140},{16,144},{20,148},{24,152},{28,15... | collective-permute-start | bytes 61448 | tf_op jit(solution)/shard_map/ppermute | solution.py:515
  27.2 81.5 %all-to-all-start = ((bf16[256,11,4,128]{3,2,1,0:T(4,128)(2,1)}), bf16[256,11,4,128]{3,2,1,0:T(4,128)(2,1)}, u32[]{:S(2)}, u32[]{:S(2)}) async-start(bf16[256,11,4,128]{3,2,1,0:T(4,128)(2,1)} %bitcast.5), calls=%async_computation | async-start | bytes 5767168 | tf_op jit(solution)/shard_map/all_to_all | solution.py:526
  40.2 148.6 %all-gather.5.cloned.1.call-start = ((), (), s32[]{:S(2)}) async-start(), calls=%async_computation.4 | async-start | bytes 6553600 | tf_op jit(solution)/shard_map/all_gather | solution.py:539
  40.4 9.3 %collective-permute-start.4 = (s32[2,128]{1,0:T(2,128)S(1)}, s32[2,128]{1,0:T(2,128)S(1)}, u32[]{:S(2)}, u32[]{:S(2)}) collective-permute-start(s32[2,128]{1,0:T(2,128)S(1)} %pad_add_fusion), channel_id=1, source_target_pairs={{0,3},{1,0},{2,1},{3,2},{4,7},{5,4},{6,5},{7,6},{8,11},{9,8},{10,9... | collective-permute-start | bytes 3080 | tf_op jit(solution)/shard_map/ppermute | solution.py:481
  43.3 7.3 %collective-permute-start.5 = (s32[2,128]{1,0:T(2,128)S(1)}, s32[2,128]{1,0:T(2,128)S(1)}, u32[]{:S(2)}, u32[]{:S(2)}) collective-permute-start(s32[2,128]{1,0:T(2,128)S(1)} %pad_add_fusion), channel_id=1, source_target_pairs={{0,2},{1,3},{2,0},{3,1},{4,6},{5,7},{6,4},{7,5},{8,10},{9,11},{10,... | collective-permute-start | bytes 3080 | tf_op jit(solution)/shard_map/ppermute | solution.py:481
  44.1 6.6 %collective-permute-start.6 = (s32[2,128]{1,0:T(2,128)S(1)}, s32[2,128]{1,0:T(2,128)S(1)}, u32[]{:S(2)}, u32[]{:S(2)}) collective-permute-start(s32[2,128]{1,0:T(2,128)S(1)} %pad_add_fusion), channel_id=1, source_target_pairs={{0,1},{1,2},{2,3},{3,0},{4,5},{5,6},{6,7},{7,4},{8,9},{9,10},{10,1... | collective-permute-start | bytes 3080 | tf_op jit(solution)/shard_map/ppermute | solution.py:481
  45.6 12.2 %collective-permute-start.10 = (bf16[8,80,128]{2,1,0:T(8,128)(2,1)S(1)}, bf16[8,80,128]{2,1,0:T(8,128)(2,1)S(1)}, u32[]{:S(2)}, u32[]{:S(2)}) collective-permute-start(bf16[8,80,128]{2,1,0:T(8,128)(2,1)S(1)} %constant_dynamic-update-slice_fusion.refs_0_), channel_id=1, source_target_pairs={{0,16},{4,20},{8,24},{12,28},{16,0},{20,4},{24,8},{28,12},{32,48},... | collective-permute-start | bytes 491528 | tf_op jit(solution)/shard_map/ppermute | solution.py:473
  48.6 14.0 %collective-permute-start.12 = (bf16[8,80,128]{2,1,0:T(8,128)(2,1)S(1)}, bf16[8,80,128]{2,1,0:T(8,128)(2,1)S(1)}, u32[]{:S(2)}, u32[]{:S(2)}) collective-permute-start(bf16[8,80,128]{2,1,0:T(8,128)(2,1)S(1)} %constant_dynamic-update-slice_fusion.refs_0_), channel_id=1, source_target_pairs={{0,24},{4,28},{8,0},{12,4},{16,8},{20,12},{24,16},{28,20},{32,56},... | collective-permute-start | bytes 491528 | tf_op jit(solution)/shard_map/ppermute | solution.py:473
  49.7 13.1 %collective-permute-start.8 = (bf16[8,80,128]{2,1,0:T(8,128)(2,1)S(1)}, bf16[8,80,128]{2,1,0:T(8,128)(2,1)S(1)}, u32[]{:S(2)}, u32[]{:S(2)}) collective-permute-start(bf16[8,80,128]{2,1,0:T(8,128)(2,1)S(1)} %constant_dynamic-update-slice_fusion.refs_0_), channel_id=1, source_target_pairs={{0,8},{4,12},{8,16},{12,20},{16,24},{20,28},{24,0},{28,4},{32,40},... | collective-permute-start | bytes 491528 | tf_op jit(solution)/shard_map/ppermute | solution.py:473
  50.6 13.0 %collective-permute-start.7 = (bf16[8,80,128]{2,1,0:T(8,128)(2,1)S(1)}, bf16[8,80,128]{2,1,0:T(8,128)(2,1)S(1)}, u32[]{:S(2)}, u32[]{:S(2)}) collective-permute-start(bf16[8,80,128]{2,1,0:T(8,128)(2,1)S(1)} %constant_dynamic-update-slice_fusion.refs_0_), channel_id=1, source_target_pairs={{0,4},{4,0},{8,12},{12,8},{16,20},{20,16},{24,28},{28,24},{32,36},... | collective-permute-start | bytes 491528 | tf_op jit(solution)/shard_map/ppermute | solution.py:477
  57.8 5.9 %collective-permute-start.11 = (bf16[8,80,128]{2,1,0:T(8,128)(2,1)S(1)}, bf16[8,80,128]{2,1,0:T(8,128)(2,1)S(1)}, u32[]{:S(2)}, u32[]{:S(2)}) collective-permute-start(bf16[8,80,128]{2,1,0:T(8,128)(2,1)S(1)} %collective-permute-done.10.refs_4_), channel_id=1, source_target_pairs={{0,4},{4,0},{8,12},{12,8},{16,20},{20,16},{24,28},{28,24},{32,36},... | collective-permute-start | bytes 491528 | tf_op jit(solution)/shard_map/ppermute | solution.py:477
  116.6 26.8 %all-to-all-start.1 = ((bf16[64,32,128]{2,1,0:T(8,128)(2,1)}), bf16[64,32,128]{2,1,0:T(8,128)(2,1)S(1)}, u32[]{:S(2)}, u32[]{:S(2)}) async-start(bf16[64,32,128]{2,1,0:T(8,128)(2,1)} %get-tuple-element.41), calls=%async_computation.1 | async-start | bytes 1048576 | tf_op jit(solution)/shard_map/all_to_all | solution.py:543
  149.5 50.3 %all-to-all-start.2 = ((bf16[256,24,128]{2,1,0:T(8,128)(2,1)}), bf16[256,24,128]{2,1,0:T(8,128)(2,1)S(1)}, u32[]{:S(2)}, u32[]{:S(2)}) async-start(bf16[256,24,128]{2,1,0:T(8,128)(2,1)} %bitcast.25), calls=%async_computation.2 | async-start | bytes 3145728 | tf_op jit(solution)/shard_map/all_to_all | solution.py:550
  166.2 5.6 %collective-permute-start.14 = (bf16[4,8,80,128]{3,2,1,0:T(8,128)(2,1)}, bf16[4,8,80,128]{3,2,1,0:T(8,128)(2,1)S(1)}, u32[]{:S(2)}, u32[]{:S(2)}) collective-permute-start(bf16[4,8,80,128]{3,2,1,0:T(8,128)(2,1)} %dynamic-slice_bitcast_fusion), channel_id=1, source_target_pairs={{0,4},{4,0},{8,12},{12,8},{16,20},{20,16},{24,28},{28,24},{32,36},... | collective-permute-start | bytes 1966088 | tf_op jit(solution)/shard_map/ppermute | solution.py:477
  167.2 9.1 %collective-permute-start.18 = (bf16[128,128]{1,0:T(8,128)(2,1)S(1)}, bf16[128,128]{1,0:T(8,128)(2,1)S(1)}, u32[]{:S(2)}, u32[]{:S(2)}) collective-permute-start(bf16[128,128]{1,0:T(8,128)(2,1)S(1)} %get-tuple-element.75), channel_id=1, source_target_pairs={{0,3},{1,0},{2,1},{3,2},{4,7},{5,4},{6,5},{7,6},{8,11},{9,8},{10,9... | collective-permute-start | bytes 98312 | tf_op jit(solution)/shard_map/ppermute | solution.py:481
  170.2 7.6 %collective-permute-start.19 = (bf16[128,128]{1,0:T(8,128)(2,1)S(1)}, bf16[128,128]{1,0:T(8,128)(2,1)S(1)}, u32[]{:S(2)}, u32[]{:S(2)}) collective-permute-start(bf16[128,128]{1,0:T(8,128)(2,1)S(1)} %get-tuple-element.78), channel_id=1, source_target_pairs={{0,2},{1,3},{2,0},{3,1},{4,6},{5,7},{6,4},{7,5},{8,10},{9,11},{10,... | collective-permute-start | bytes 98312 | tf_op jit(solution)/shard_map/ppermute | solution.py:481
  170.9 7.4 %collective-permute-start.20 = (bf16[128,128]{1,0:T(8,128)(2,1)S(1)}, bf16[128,128]{1,0:T(8,128)(2,1)S(1)}, u32[]{:S(2)}, u32[]{:S(2)}) collective-permute-start(bf16[128,128]{1,0:T(8,128)(2,1)S(1)} %get-tuple-element.77), channel_id=1, source_target_pairs={{0,1},{1,2},{2,3},{3,0},{4,5},{5,6},{6,7},{7,4},{8,9},{9,10},{10,1... | collective-permute-start | bytes 98312 | tf_op jit(solution)/shard_map/ppermute | solution.py:481
  172.0 10.8 %collective-permute-start.15 = (bf16[8,80,128]{2,1,0:T(8,128)(2,1)S(1)}, bf16[8,80,128]{2,1,0:T(8,128)(2,1)S(1)}, u32[]{:S(2)}, u32[]{:S(2)}) collective-permute-start(bf16[8,80,128]{2,1,0:T(8,128)(2,1)S(1)} %get-tuple-element.68), channel_id=1, source_target_pairs={{0,8},{4,12},{8,16},{12,20},{16,24},{20,28},{24,0},{28,4},{32,40},... | collective-permute-start | bytes 491528 | tf_op jit(solution)/shard_map/ppermute | solution.py:473
  173.6 15.1 %collective-permute-start.16 = (bf16[8,80,128]{2,1,0:T(8,128)(2,1)S(1)}, bf16[8,80,128]{2,1,0:T(8,128)(2,1)S(1)}, u32[]{:S(2)}, u32[]{:S(2)}) collective-permute-start(bf16[8,80,128]{2,1,0:T(8,128)(2,1)S(1)} %get-tuple-element.70), channel_id=1, source_target_pairs={{0,16},{4,20},{8,24},{12,28},{16,0},{20,4},{24,8},{28,12},{32,48},... | collective-permute-start | bytes 491528 | tf_op jit(solution)/shard_map/ppermute | solution.py:473
  176.3 12.4 %collective-permute-start.17 = (bf16[8,80,128]{2,1,0:T(8,128)(2,1)S(1)}, bf16[8,80,128]{2,1,0:T(8,128)(2,1)S(1)}, u32[]{:S(2)}, u32[]{:S(2)}) collective-permute-start(bf16[8,80,128]{2,1,0:T(8,128)(2,1)S(1)} %get-tuple-element.69), channel_id=1, source_target_pairs={{0,24},{4,28},{8,0},{12,4},{16,8},{20,12},{24,16},{28,20},{32,56},... | collective-permute-start | bytes 491528 | tf_op jit(solution)/shard_map/ppermute | solution.py:473
  204.5 9.6 %collective-permute-start.22 = (bf16[80,128]{1,0:T(8,128)(2,1)S(1)}, bf16[80,128]{1,0:T(8,128)(2,1)S(1)}, u32[]{:S(2)}, u32[]{:S(2)}) collective-permute-start(bf16[80,128]{1,0:T(8,128)(2,1)S(1)} %get-tuple-element.79), channel_id=1, source_target_pairs={{0,64},{4,68},{8,72},{12,76},{16,80},{20,84},{24,88},{28,92},{32,9... | collective-permute-start | bytes 61448 | tf_op jit(solution)/shard_map/ppermute | solution.py:515
  206.1 8.0 %collective-permute-start.23 = (bf16[80,128]{1,0:T(8,128)(2,1)S(1)}, bf16[80,128]{1,0:T(8,128)(2,1)S(1)}, u32[]{:S(2)}, u32[]{:S(2)}) collective-permute-start(bf16[80,128]{1,0:T(8,128)(2,1)S(1)} %get-tuple-element.81), channel_id=1, source_target_pairs={{0,128},{4,132},{8,136},{12,140},{16,144},{20,148},{24,152},{28,15... | collective-permute-start | bytes 61448 | tf_op jit(solution)/shard_map/ppermute | solution.py:515
  209.4 5.9 %collective-permute-start.24 = (bf16[80,128]{1,0:T(8,128)(2,1)S(1)}, bf16[80,128]{1,0:T(8,128)(2,1)S(1)}, u32[]{:S(2)}, u32[]{:S(2)}) collective-permute-start(bf16[80,128]{1,0:T(8,128)(2,1)S(1)} %get-tuple-element.80), channel_id=1, source_target_pairs={{0,192},{4,196},{8,200},{12,204},{16,208},{20,212},{24,216},{28,22... | collective-permute-start | bytes 61448 | tf_op jit(solution)/shard_map/ppermute | solution.py:515
  (36 other events, 533.1 us)
Sparse Core Ops, SparseCore 0:
  9.9 90.3 all-gather.2
  106.5 72.1 all-gather.4

commit v3 on v2

--- a/solution.py
+++ b/solution.py
@@ -562,11 +562,11 @@
         dv_parts.append(along_seq(pick(dv_view, (seq + d) % NS), d))
     grad_x = grad_x_of(in_order(dv_parts, seq), w_all.reshape(NS, -1, HEAD))
 
-    total, grad_x, dqk_back = lax.optimization_barrier((total, grad_x, dqk_back))
     half = total.astype(BF).reshape(NZ // 2, 2, *total.shape[1:])
     keep = lax.dynamic_index_in_dim(half, z % 2, 1, keepdims=False)
     give = lax.dynamic_index_in_dim(half, 1 - z % 2, 1, keepdims=False)
     half = (keep.astype(F32) + across_z(give, 1).astype(F32)).astype(BF)
+    half, grad_x, dqk_back = lax.optimization_barrier((half, grad_x, dqk_back))
     total = pick(half, z // 2).astype(F32)
     for bits in (1, 2, 3):
         total = total + across_z(pick(half, (z // 2) ^ bits), 2 * bits).astype(F32)

time: 231 us -> 231 us (level)
  waiting for transfers between devices: 88.7 us -> 83.7 us
  starting transfers between devices: 72.2 us -> 76.3 us
    all_to_all x1, waiting for transfers between devices: 4.87 us -> 0.91 us  [shards(): lax.all_to_all(dqk_out.reshape(NDP * NS, 24, HEAD), ('dp', 'seq'), split_...]
    ppermute x6, waiting for transfers between devices: 21.8 us -> 18.5 us  [along_x(): lax.ppermute(value, 'dp', [(dp_of(z, x, c), dp_of(z, (x + d) % NX, c)) fo...]
  transfers between devices with their start and end apart: 33 -> 33, of which waited for: 20 -> 18; matrix products, arithmetic and copies ran while one was open for 3% -> 3% of each run, Pallas kernels for 20% -> 20%
where the time goes in v3:
time: 231 us; the launch traced here: 230 us
  waiting for transfers between devices  83.7 us (36%)
  starting transfers between devices  76.3 us (33%)
  Pallas kernels  46.6 us (20%)
  between operations  14.6 us (6%)
  local copies, waits for them, and re-layouts  4.47 us (2%)
  other arithmetic  4.03 us (2%)
    all_gather x1, waiting for transfers between devices, shards(): x_all = lax.all_gather(x_saved, 'seq', axis=0, tiled=True)  36 us
    ppermute x8, starting transfers between devices, across_z(): return lax.ppermute(value, 'dp', swap)  19.3 us
    ppermute x6, waiting for transfers between devices, along_x(): lax.ppermute(value, 'dp', [(dp_of(z, x, c), dp_of(z, (x + d) % NX, c)) fo...  18.5 us
    ppermute x9, starting transfers between devices, along_seq(): return lax.ppermute(value, 'seq', [(s, (s + d) % NS) for s in range(NS)])  13.8 us
    all_to_all x1, starting transfers between devices, shards(): lax.all_to_all(rows.reshape(NDP * NS, 11, CAP, HEAD), ('dp', 'seq'), spli...  13 us
    ppermute x6, starting transfers between devices, along_x(): lax.ppermute(value, 'dp', [(dp_of(z, x, c), dp_of(z, (x + d) % NX, c)) fo...  10.7 us
    all_to_all x1, starting transfers between devices, shards(): both = lax.all_to_all(both, 'dp', split_axis=0, concat_axis=0, tiled=True)  10 us
    ppermute x8, waiting for transfers between devices, across_z(): return lax.ppermute(value, 'dp', swap)  9.61 us
  transfers between devices with their start and end apart: 33, of which 18 were waited for; matrix products, arithmetic and copies ran while one was open for 3% of the time, Pallas kernels for 20%

profile of v3, /device:TPU:32, one launch (start us, length us, event | category | flops | bytes accessed | tf_op | source)
XLA Modules:
  0.0 229.7 jit_solution(13321903048999535656)
XLA Ops:
  8.7 6.3 %collective-permute-start = (bf16[80,128]{1,0:T(8,128)(2,1)S(1)}, bf16[80,128]{1,0:T(8,128)(2,1)S(1)}, u32[]{:S(2)}, u32[]{:S(2)}) collective-permute-start(bf16[80,128]{1,0:T(8,128)(2,1)S(1)} %constant_dynamic-slice_fusion), channel_id=1, source_target_pairs={{0,128},{4,132},{8,136},{12,140},{16,144},{20,148},{24,152},{28,15... | collective-permute-start | bytes 61448 | tf_op jit(solution)/shard_map/ppermute | solution.py:515
  16.3 3.8 %pack_rows.1 = bf16[64,4,11,4,128]{4,3,2,1,0:T(4,128)(2,1)} custom-call(s32[1,128]{1,0:T(1,128)S(1)} %add_bitcast_fusion.1.slots_ref.slot_ref, f32[1,128]{1,0:T(1,128)S(1)} %bitcast.70, bf16[128,2560]{1,0:T(8,128)(2,1)S(1)} %copy-done.3, bf16[128,512]{1,0:T(8,128)(2,1)S(1)} %copy-done.5, bf16[128,2560]{1,0:T(8,128)(2,1)S(1)} %copy-done.4), custom_call_target="tpu_custom_call" | custom-call | flops 1600000000 | bytes 5000000 | tf_op jit(solution)/shard_map/pack_rows/pallas_call | solution.py:100
  27.2 13.0 %all-to-all-start = ((bf16[256,11,4,128]{3,2,1,0:T(4,128)(2,1)}), bf16[256,11,4,128]{3,2,1,0:T(4,128)(2,1)}, u32[]{:S(2)}, u32[]{:S(2)}) async-start(bf16[256,11,4,128]{3,2,1,0:T(4,128)(2,1)} %bitcast.5), calls=%async_computation | async-start | bytes 5767168 | tf_op jit(solution)/shard_map/all_to_all | solution.py:526
  40.4 3.0 %collective-permute-start.4 = (s32[2,128]{1,0:T(2,128)S(1)}, s32[2,128]{1,0:T(2,128)S(1)}, u32[]{:S(2)}, u32[]{:S(2)}) collective-permute-start(s32[2,128]{1,0:T(2,128)S(1)} %pad_add_fusion), channel_id=1, source_target_pairs={{0,3},{1,0},{2,1},{3,2},{4,7},{5,4},{6,5},{7,6},{8,11},{9,8},{10,9... | collective-permute-start | bytes 3080 | tf_op jit(solution)/shard_map/ppermute | solution.py:481
  45.6 3.0 %collective-permute-start.10 = (bf16[8,80,128]{2,1,0:T(8,128)(2,1)S(1)}, bf16[8,80,128]{2,1,0:T(8,128)(2,1)S(1)}, u32[]{:S(2)}, u32[]{:S(2)}) collective-permute-start(bf16[8,80,128]{2,1,0:T(8,128)(2,1)S(1)} %constant_dynamic-update-slice_fusion.refs_0_), channel_id=1, source_target_pairs={{0,16},{4,20},{8,24},{12,28},{16,0},{20,4},{24,8},{28,12},{32,48},... | collective-permute-start | bytes 491528 | tf_op jit(solution)/shard_map/ppermute | solution.py:473
  50.7 7.1 %collective-permute-done.10.refs_4_ = bf16[8,80,128]{2,1,0:T(8,128)(2,1)S(1)} collective-permute-done((bf16[8,80,128]{2,1,0:T(8,128)(2,1)S(1)}, bf16[8,80,128]{2,1,0:T(8,128)(2,1)S(1)}, u32[]{:S(2)}, u32[]{:S(2)}) %collective-permute-start.10) | collective-permute-done | bytes 163872 | tf_op jit(solution)/shard_map/ppermute | solution.py:473
  57.8 4.8 %collective-permute-done.12.refs_6_ = bf16[8,80,128]{2,1,0:T(8,128)(2,1)S(1)} collective-permute-done((bf16[8,80,128]{2,1,0:T(8,128)(2,1)S(1)}, bf16[8,80,128]{2,1,0:T(8,128)(2,1)S(1)}, u32[]{:S(2)}, u32[]{:S(2)}) %collective-permute-start.12) | collective-permute-done | bytes 163872 | tf_op jit(solution)/shard_map/ppermute | solution.py:473
  64.2 36.0 %all-gather.3.cloned.1.call-done.x_ref = bf16[512,5120]{1,0:T(8,128)(2,1)} async-done(((bf16[128,5120]{1,0:T(8,128)(2,1)}), bf16[512,5120]{1,0:T(8,128)(2,1)}) %all-gather.3.cloned.1.call-update) | async-done | bytes 5242896 | tf_op jit(solution)/shard_map/all_gather | solution.py:532
  100.3 6.1 %values.1 = (bf16[64,16,128]{2,1,0:T(8,128)(2,1)}, bf16[5120,128]{1,0:T(8,128)(2,1)}) custom-call(s32[3]{0:T(128)} %pad_add_fusion.1.place_ref, s32[4,128]{1,0:T(4,128)} %get-tuple-element.50.slot_ref, bf16[512,5120]{1,0:T(8,128)(2,1)} %all-gather.3.cloned.1.call-done.x_ref, bf16[8,80,128]{2,1,0:T(8,128)(2,1)} %copy-done.16, bf16[8,80,128]{2,1,0:T(8,128)(2,1)} %copy-done.20, ...), custom_call_target="tpu_custom_call" | custom-call | flops 800000000 | bytes 8000000 | tf_op jit(solution)/shard_map/values/pallas_call | solution.py:144
  108.7 7.9 %probs.1 = (bf16[64,32,128]{2,1,0:T(8,128)(2,1)}, bf16[4,640,128]{2,1,0:T(8,128)(2,1)}, bf16[512,128]{1,0:T(8,128)(2,1)}, bf16[4,640,128]{2,1,0:T(8,128)(2,1)}, ...) custom-call(s32[3]{0:T(128)} %bitcast.76, ...), custom_call_target="tpu_custom_call" | custom-call | flops 3000000000 | bytes 9000000 | tf_op jit(solution)/shard_map/probs/pallas_call | solution.py:256
  116.6 10.0 %all-to-all-start.1 = ((bf16[64,32,128]{2,1,0:T(8,128)(2,1)}), bf16[64,32,128]{2,1,0:T(8,128)(2,1)S(1)}, u32[]{:S(2)}, u32[]{:S(2)}) async-start(bf16[64,32,128]{2,1,0:T(8,128)(2,1)} %get-tuple-element.41), calls=%async_computation.1 | async-start | bytes 1048576 | tf_op jit(solution)/shard_map/all_to_all | solution.py:543
  126.8 8.0 %turn.1.x_ref = bf16[5120,512]{1,0:T(8,128)(2,1)} custom-call(bf16[512,5120]{1,0:T(8,128)(2,1)} %all-gather.3.cloned.1.call-done.x_ref), custom_call_target="tpu_custom_call" | custom-call | flops 1000000 | bytes 11000000 | tf_op jit(solution)/shard_map/turn/pallas_call | solution.py:165
  134.7 8.7 %all-to-all-done.1.r_ref = bf16[64,32,128]{2,1,0:T(8,128)(2,1)S(1)} async-done(((bf16[64,32,128]{2,1,0:T(8,128)(2,1)}), bf16[64,32,128]{2,1,0:T(8,128)(2,1)S(1)}, u32[]{:S(2)}, u32[]{:S(2)}) %all-to-all-start.1) | async-done | bytes 524320 | tf_op jit(solution)/shard_map/all_to_all | solution.py:543
  143.5 6.0 %grads.1 = bf16[64,4,24,128]{3,2,1,0:T(8,128)(2,1)} custom-call(s32[4,128]{1,0:T(4,128)S(1)} %copy-done.1, bf16[64,32,128]{2,1,0:T(8,128)(2,1)S(1)} %all-to-all-done.1.r_ref, bf16[4,640,128]{2,1,0:T(8,128)(2,1)S(1)} %copy-done.7, bf16[512,128]{1,0:T(8,128)(2,1)S(1)} %copy-done.13, bf16[4,640,128]{2,1,0:T(8,128)(2,1)S(1)} %copy-done.8, ...), custom_call_target="tpu_custom_call" | custom-call | flops 3000000000 | bytes 8000000 | tf_op jit(solution)/shard_map/grads/pallas_call | solution.py:329
  149.5 8.9 %all-to-all-start.2 = ((bf16[256,24,128]{2,1,0:T(8,128)(2,1)}), bf16[256,24,128]{2,1,0:T(8,128)(2,1)S(1)}, u32[]{:S(2)}, u32[]{:S(2)}) async-start(bf16[256,24,128]{2,1,0:T(8,128)(2,1)} %bitcast.28), calls=%async_computation.2 | async-start | bytes 3145728 | tf_op jit(solution)/shard_map/all_to_all | solution.py:550
  158.4 5.7 %weight_terms.1 = (bf16[512,128]{1,0:T(8,128)(2,1)}, bf16[2,4,8,80,128]{4,3,2,1,0:T(8,128)(2,1)}) custom-call(s32[4,128]{1,0:T(4,128)} %get-tuple-element.50.slot_ref, bf16[64,32,128]{2,1,0:T(8,128)(2,1)} %copy-done, bf16[5120,512]{1,0:T(8,128)(2,1)} %turn.1.x_ref), custom_call_target="tpu_custom_call" | custom-call | flops 800000000 | bytes 7000000 | tf_op jit(solution)/shard_map/weight_terms/pallas_call | solution.py:375
  175.6 3.0 %collective-permute-start.19 = (bf16[128,128]{1,0:T(8,128)(2,1)S(1)}, bf16[128,128]{1,0:T(8,128)(2,1)S(1)}, u32[]{:S(2)}, u32[]{:S(2)}) collective-permute-start(bf16[128,128]{1,0:T(8,128)(2,1)S(1)} %get-tuple-element.75), channel_id=1, source_target_pairs={{0,3},{1,0},{2,1},{3,2},{4,7},{5,4},{6,5},{7,6},{8,11},{9,8},{10,9... | collective-permute-start | bytes 98312 | tf_op jit(solution)/shard_map/ppermute | solution.py:481
  180.2 6.4 %collective-permute-done.16 = bf16[8,80,128]{2,1,0:T(8,128)(2,1)S(1)} collective-permute-done((bf16[8,80,128]{2,1,0:T(8,128)(2,1)S(1)}, bf16[8,80,128]{2,1,0:T(8,128)(2,1)S(1)}, u32[]{:S(2)}, u32[]{:S(2)}) %collective-permute-start.16) | collective-permute-done | bytes 163872 | tf_op jit(solution)/shard_map/ppermute | solution.py:473
  189.2 3.5 %collective-permute-done.18 = bf16[4,80,128]{2,1,0:T(8,128)(2,1)S(1)} collective-permute-done((bf16[4,80,128]{2,1,0:T(8,128)(2,1)S(1)}, bf16[4,80,128]{2,1,0:T(8,128)(2,1)S(1)}, u32[]{:S(2)}, u32[]{:S(2)}) %collective-permute-start.18) | collective-permute-done | bytes 81952 | tf_op jit(solution)/shard_map/ppermute | solution.py:515
  192.8 6.1 %grad_x.1 = bf16[128,5120]{1,0:T(8,128)(2,1)} custom-call(bf16[4,128,128]{2,1,0:T(8,128)(2,1)} %select_select_fusion.1.dv_ref, bf16[4,5120,128]{2,1,0:T(8,128)(2,1)} %bitcast.71), custom_call_target="tpu_custom_call" | custom-call | flops 700000000 | bytes 7000000 | tf_op jit(solution)/shard_map/grad_x/pallas_call | solution.py:406
  202.2 5.0 %collective-permute-start.23 = (bf16[80,128]{1,0:T(8,128)(2,1)S(1)}, bf16[80,128]{1,0:T(8,128)(2,1)S(1)}, u32[]{:S(2)}, u32[]{:S(2)}) collective-permute-start(bf16[80,128]{1,0:T(8,128)(2,1)S(1)} %get-tuple-element.81), channel_id=1, source_target_pairs={{0,128},{4,132},{8,136},{12,140},{16,144},{20,148},{24,152},{28,15... | collective-permute-start | bytes 61448 | tf_op jit(solution)/shard_map/ppermute | solution.py:515
  207.3 3.1 %unpack.1 = (bf16[128,2560]{1,0:T(8,128)(2,1)}, bf16[128,512]{1,0:T(8,128)(2,1)}) custom-call(s32[1,128]{1,0:T(1,128)} %copy-done.2, bf16[64,4,24,128]{3,2,1,0:T(8,128)(2,1)} %bitcast.72), custom_call_target="tpu_custom_call" | custom-call | flops 500000000 | bytes 4000000 | tf_op jit(solution)/shard_map/unpack/pallas_call | solution.py:447
  213.2 2.9 %collective-permute-start.25 = (f32[80,128]{1,0:T(8,128)S(1)}, f32[80,128]{1,0:T(8,128)S(1)}, u32[]{:S(2)}, u32[]{:S(2)}) collective-permute-start(f32[80,128]{1,0:T(8,128)S(1)} %fusion.8), channel_id=1, source_target_pairs={{0,3},{1,0},{2,1},{3,2},{4,7},{5,4},{6,5},{7,6},{8,11},{9,8},{10,9... | collective-permute-start | bytes 122888 | tf_op jit(solution)/shard_map/ppermute | solution.py:481
  217.8 3.8 %collective-permute-done.26 = f32[80,128]{1,0:T(8,128)S(1)} collective-permute-done((f32[80,128]{1,0:T(8,128)S(1)}, f32[80,128]{1,0:T(8,128)S(1)}, u32[]{:S(2)}, u32[]{:S(2)}) %collective-permute-start.26) | collective-permute-done | bytes 40992 | tf_op jit(solution)/shard_map/ppermute | solution.py:481
  (137 shorter events, 43.1 us)
Async XLA Ops:
  7.2 93.1 %all-gather.3.cloned.1.call-start = ((), (), s32[]{:S(2)}) async-start(), calls=%async_computation.3 | async-start | bytes 6553600 | tf_op jit(solution)/shard_map/all_gather | solution.py:532
  8.7 11.4 %collective-permute-start = (bf16[80,128]{1,0:T(8,128)(2,1)S(1)}, bf16[80,128]{1,0:T(8,128)(2,1)S(1)}, u32[]{:S(2)}, u32[]{:S(2)}) collective-permute-start(bf16[80,128]{1,0:T(8,128)(2,1)S(1)} %constant_dynamic-slice_fusion), channel_id=1, source_target_pairs={{0,128},{4,132},{8,136},{12,140},{16,144},{20,148},{24,152},{28,15... | collective-permute-start | bytes 61448 | tf_op jit(solution)/shard_map/ppermute | solution.py:515
  27.2 81.5 %all-to-all-start = ((bf16[256,11,4,128]{3,2,1,0:T(4,128)(2,1)}), bf16[256,11,4,128]{3,2,1,0:T(4,128)(2,1)}, u32[]{:S(2)}, u32[]{:S(2)}) async-start(bf16[256,11,4,128]{3,2,1,0:T(4,128)(2,1)} %bitcast.5), calls=%async_computation | async-start | bytes 5767168 | tf_op jit(solution)/shard_map/all_to_all | solution.py:526
  40.2 152.6 %all-gather.5.cloned.1.call-start = ((), (), s32[]{:S(2)}) async-start(), calls=%async_computation.4 | async-start | bytes 6553600 | tf_op jit(solution)/shard_map/all_gather | solution.py:539
  40.4 9.3 %collective-permute-start.4 = (s32[2,128]{1,0:T(2,128)S(1)}, s32[2,128]{1,0:T(2,128)S(1)}, u32[]{:S(2)}, u32[]{:S(2)}) collective-permute-start(s32[2,128]{1,0:T(2,128)S(1)} %pad_add_fusion), channel_id=1, source_target_pairs={{0,3},{1,0},{2,1},{3,2},{4,7},{5,4},{6,5},{7,6},{8,11},{9,8},{10,9... | collective-permute-start | bytes 3080 | tf_op jit(solution)/shard_map/ppermute | solution.py:481
  43.3 7.3 %collective-permute-start.5 = (s32[2,128]{1,0:T(2,128)S(1)}, s32[2,128]{1,0:T(2,128)S(1)}, u32[]{:S(2)}, u32[]{:S(2)}) collective-permute-start(s32[2,128]{1,0:T(2,128)S(1)} %pad_add_fusion), channel_id=1, source_target_pairs={{0,2},{1,3},{2,0},{3,1},{4,6},{5,7},{6,4},{7,5},{8,10},{9,11},{10,... | collective-permute-start | bytes 3080 | tf_op jit(solution)/shard_map/ppermute | solution.py:481
  44.1 6.6 %collective-permute-start.6 = (s32[2,128]{1,0:T(2,128)S(1)}, s32[2,128]{1,0:T(2,128)S(1)}, u32[]{:S(2)}, u32[]{:S(2)}) collective-permute-start(s32[2,128]{1,0:T(2,128)S(1)} %pad_add_fusion), channel_id=1, source_target_pairs={{0,1},{1,2},{2,3},{3,0},{4,5},{5,6},{6,7},{7,4},{8,9},{9,10},{10,1... | collective-permute-start | bytes 3080 | tf_op jit(solution)/shard_map/ppermute | solution.py:481
  45.6 12.2 %collective-permute-start.10 = (bf16[8,80,128]{2,1,0:T(8,128)(2,1)S(1)}, bf16[8,80,128]{2,1,0:T(8,128)(2,1)S(1)}, u32[]{:S(2)}, u32[]{:S(2)}) collective-permute-start(bf16[8,80,128]{2,1,0:T(8,128)(2,1)S(1)} %constant_dynamic-update-slice_fusion.refs_0_), channel_id=1, source_target_pairs={{0,16},{4,20},{8,24},{12,28},{16,0},{20,4},{24,8},{28,12},{32,48},... | collective-permute-start | bytes 491528 | tf_op jit(solution)/shard_map/ppermute | solution.py:473
  48.6 14.0 %collective-permute-start.12 = (bf16[8,80,128]{2,1,0:T(8,128)(2,1)S(1)}, bf16[8,80,128]{2,1,0:T(8,128)(2,1)S(1)}, u32[]{:S(2)}, u32[]{:S(2)}) collective-permute-start(bf16[8,80,128]{2,1,0:T(8,128)(2,1)S(1)} %constant_dynamic-update-slice_fusion.refs_0_), channel_id=1, source_target_pairs={{0,24},{4,28},{8,0},{12,4},{16,8},{20,12},{24,16},{28,20},{32,56},... | collective-permute-start | bytes 491528 | tf_op jit(solution)/shard_map/ppermute | solution.py:473
  49.7 13.1 %collective-permute-start.8 = (bf16[8,80,128]{2,1,0:T(8,128)(2,1)S(1)}, bf16[8,80,128]{2,1,0:T(8,128)(2,1)S(1)}, u32[]{:S(2)}, u32[]{:S(2)}) collective-permute-start(bf16[8,80,128]{2,1,0:T(8,128)(2,1)S(1)} %constant_dynamic-update-slice_fusion.refs_0_), channel_id=1, source_target_pairs={{0,8},{4,12},{8,16},{12,20},{16,24},{20,28},{24,0},{28,4},{32,40},... | collective-permute-start | bytes 491528 | tf_op jit(solution)/shard_map/ppermute | solution.py:473
  50.6 13.0 %collective-permute-start.7 = (bf16[8,80,128]{2,1,0:T(8,128)(2,1)S(1)}, bf16[8,80,128]{2,1,0:T(8,128)(2,1)S(1)}, u32[]{:S(2)}, u32[]{:S(2)}) collective-permute-start(bf16[8,80,128]{2,1,0:T(8,128)(2,1)S(1)} %constant_dynamic-update-slice_fusion.refs_0_), channel_id=1, source_target_pairs={{0,4},{4,0},{8,12},{12,8},{16,20},{20,16},{24,28},{28,24},{32,36},... | collective-permute-start | bytes 491528 | tf_op jit(solution)/shard_map/ppermute | solution.py:477
  57.8 5.9 %collective-permute-start.11 = (bf16[8,80,128]{2,1,0:T(8,128)(2,1)S(1)}, bf16[8,80,128]{2,1,0:T(8,128)(2,1)S(1)}, u32[]{:S(2)}, u32[]{:S(2)}) collective-permute-start(bf16[8,80,128]{2,1,0:T(8,128)(2,1)S(1)} %collective-permute-done.10.refs_4_), channel_id=1, source_target_pairs={{0,4},{4,0},{8,12},{12,8},{16,20},{20,16},{24,28},{28,24},{32,36},... | collective-permute-start | bytes 491528 | tf_op jit(solution)/shard_map/ppermute | solution.py:477
  116.6 26.8 %all-to-all-start.1 = ((bf16[64,32,128]{2,1,0:T(8,128)(2,1)}), bf16[64,32,128]{2,1,0:T(8,128)(2,1)S(1)}, u32[]{:S(2)}, u32[]{:S(2)}) async-start(bf16[64,32,128]{2,1,0:T(8,128)(2,1)} %get-tuple-element.41), calls=%async_computation.1 | async-start | bytes 1048576 | tf_op jit(solution)/shard_map/all_to_all | solution.py:543
  149.5 50.2 %all-to-all-start.2 = ((bf16[256,24,128]{2,1,0:T(8,128)(2,1)}), bf16[256,24,128]{2,1,0:T(8,128)(2,1)S(1)}, u32[]{:S(2)}, u32[]{:S(2)}) async-start(bf16[256,24,128]{2,1,0:T(8,128)(2,1)} %bitcast.28), calls=%async_computation.2 | async-start | bytes 3145728 | tf_op jit(solution)/shard_map/all_to_all | solution.py:550
  169.0 10.2 %collective-permute-start.15 = (bf16[8,80,128]{2,1,0:T(8,128)(2,1)S(1)}, bf16[8,80,128]{2,1,0:T(8,128)(2,1)S(1)}, u32[]{:S(2)}, u32[]{:S(2)}) collective-permute-start(bf16[8,80,128]{2,1,0:T(8,128)(2,1)S(1)} %get-tuple-element.68), channel_id=1, source_target_pairs={{0,8},{4,12},{8,16},{12,20},{16,24},{20,28},{24,0},{28,4},{32,40},... | collective-permute-start | bytes 491528 | tf_op jit(solution)/shard_map/ppermute | solution.py:473
  170.6 15.9 %collective-permute-start.16 = (bf16[8,80,128]{2,1,0:T(8,128)(2,1)S(1)}, bf16[8,80,128]{2,1,0:T(8,128)(2,1)S(1)}, u32[]{:S(2)}, u32[]{:S(2)}) collective-permute-start(bf16[8,80,128]{2,1,0:T(8,128)(2,1)S(1)} %get-tuple-element.70), channel_id=1, source_target_pairs={{0,16},{4,20},{8,24},{12,28},{16,0},{20,4},{24,8},{28,12},{32,48},... | collective-permute-start | bytes 491528 | tf_op jit(solution)/shard_map/ppermute | solution.py:473
  173.3 13.2 %collective-permute-start.17 = (bf16[8,80,128]{2,1,0:T(8,128)(2,1)S(1)}, bf16[8,80,128]{2,1,0:T(8,128)(2,1)S(1)}, u32[]{:S(2)}, u32[]{:S(2)}) collective-permute-start(bf16[8,80,128]{2,1,0:T(8,128)(2,1)S(1)} %get-tuple-element.69), channel_id=1, source_target_pairs={{0,24},{4,28},{8,0},{12,4},{16,8},{20,12},{24,16},{28,20},{32,56},... | collective-permute-start | bytes 491528 | tf_op jit(solution)/shard_map/ppermute | solution.py:473
  175.6 12.9 %collective-permute-start.19 = (bf16[128,128]{1,0:T(8,128)(2,1)S(1)}, bf16[128,128]{1,0:T(8,128)(2,1)S(1)}, u32[]{:S(2)}, u32[]{:S(2)}) collective-permute-start(bf16[128,128]{1,0:T(8,128)(2,1)S(1)} %get-tuple-element.75), channel_id=1, source_target_pairs={{0,3},{1,0},{2,1},{3,2},{4,7},{5,4},{6,5},{7,6},{8,11},{9,8},{10,9... | collective-permute-start | bytes 98312 | tf_op jit(solution)/shard_map/ppermute | solution.py:481
  178.5 9.9 %collective-permute-start.20 = (bf16[128,128]{1,0:T(8,128)(2,1)S(1)}, bf16[128,128]{1,0:T(8,128)(2,1)S(1)}, u32[]{:S(2)}, u32[]{:S(2)}) collective-permute-start(bf16[128,128]{1,0:T(8,128)(2,1)S(1)} %get-tuple-element.78), channel_id=1, source_target_pairs={{0,2},{1,3},{2,0},{3,1},{4,6},{5,7},{6,4},{7,5},{8,10},{9,11},{10,... | collective-permute-start | bytes 98312 | tf_op jit(solution)/shard_map/ppermute | solution.py:481
  179.3 9.2 %collective-permute-start.21 = (bf16[128,128]{1,0:T(8,128)(2,1)S(1)}, bf16[128,128]{1,0:T(8,128)(2,1)S(1)}, u32[]{:S(2)}, u32[]{:S(2)}) collective-permute-start(bf16[128,128]{1,0:T(8,128)(2,1)S(1)} %get-tuple-element.77), channel_id=1, source_target_pairs={{0,1},{1,2},{2,3},{3,0},{4,5},{5,6},{6,7},{7,4},{8,9},{9,10},{10,1... | collective-permute-start | bytes 98312 | tf_op jit(solution)/shard_map/ppermute | solution.py:481
  186.6 6.1 %collective-permute-start.18 = (bf16[4,80,128]{2,1,0:T(8,128)(2,1)S(1)}, bf16[4,80,128]{2,1,0:T(8,128)(2,1)S(1)}, u32[]{:S(2)}, u32[]{:S(2)}) collective-permute-start(bf16[4,80,128]{2,1,0:T(8,128)(2,1)S(1)} %dynamic-slice_bitcast_fusion.4), channel_id=1, source_target_pairs={{0,32},{4,36},{8,40},{12,44},{16,48},{20,52},{24,56},{28,60},{32,0... | collective-permute-start | bytes 245768 | tf_op jit(solution)/shard_map/ppermute | solution.py:515
  199.8 10.6 %collective-permute-start.22 = (bf16[80,128]{1,0:T(8,128)(2,1)S(1)}, bf16[80,128]{1,0:T(8,128)(2,1)S(1)}, u32[]{:S(2)}, u32[]{:S(2)}) collective-permute-start(bf16[80,128]{1,0:T(8,128)(2,1)S(1)} %get-tuple-element.79), channel_id=1, source_target_pairs={{0,64},{4,68},{8,72},{12,76},{16,80},{20,84},{24,88},{28,92},{32,9... | collective-permute-start | bytes 61448 | tf_op jit(solution)/shard_map/ppermute | solution.py:515
  202.2 8.1 %collective-permute-start.23 = (bf16[80,128]{1,0:T(8,128)(2,1)S(1)}, bf16[80,128]{1,0:T(8,128)(2,1)S(1)}, u32[]{:S(2)}, u32[]{:S(2)}) collective-permute-start(bf16[80,128]{1,0:T(8,128)(2,1)S(1)} %get-tuple-element.81), channel_id=1, source_target_pairs={{0,128},{4,132},{8,136},{12,140},{16,144},{20,148},{24,152},{28,15... | collective-permute-start | bytes 61448 | tf_op jit(solution)/shard_map/ppermute | solution.py:515
  207.3 5.9 %collective-permute-start.24 = (bf16[80,128]{1,0:T(8,128)(2,1)S(1)}, bf16[80,128]{1,0:T(8,128)(2,1)S(1)}, u32[]{:S(2)}, u32[]{:S(2)}) collective-permute-start(bf16[80,128]{1,0:T(8,128)(2,1)S(1)} %get-tuple-element.80), channel_id=1, source_target_pairs={{0,192},{4,196},{8,200},{12,204},{16,208},{20,212},{24,216},{28,22... | collective-permute-start | bytes 61448 | tf_op jit(solution)/shard_map/ppermute | solution.py:515
  (36 other events, 523.5 us)
Sparse Core Ops, SparseCore 0:
  9.9 90.3 all-gather.2
  106.5 69.9 all-gather.4
